TPU v7x, 256 devices: a whole 4x4x8 slice. The times are simulated.
256 devices in a mesh: dp: 8 (over x, y_hi), tensor: 32 (over z, y_lo, core).
Axes of the slice: x: 4, y: 4 (y_hi: 2, y_lo: 2; y = y_hi * 2 + y_lo), z: 8, core: 2. Of those that a mesh axis runs over, the one named last changes fastest.
Arguments:
- projection_input: bfloat16 [2048, 8192], P('dp', 'tensor'), may hold values from -6 to 6
- output_gradient: bfloat16 [2048, 8192], P('dp', 'tensor'), may hold values from -6 to 6
- adapter_down: float32 [8192, 64], P('tensor'), may hold values from -0.0625 to 0.0625
- adapter_up: float32 [64, 8192], P(None, 'tensor'), may hold values from -0.75 to 0.75
- down_first_moment: float32 [8192, 64], P('tensor'), may hold values from -4 to 4
- down_second_moment: float32 [8192, 64], P('tensor'), may hold values from 0.01 to 1
- up_first_moment: float32 [64, 8192], P(None, 'tensor'), may hold values from -0.4375 to 0.4375
- up_second_moment: float32 [64, 8192], P(None, 'tensor'), may hold values from 0.0001 to 0.01
- projection_weight: bfloat16 [8192, 8192], P('tensor'), may hold values from -0.0625 to 0.0625
- queries: bfloat16 [4, 512, 8192], P(None, 'dp', 'tensor')
- stored_keys: bfloat16 [512, 128, 4096], P('dp', None, 'tensor'), as said below
- stored_values: bfloat16 [512, 128, 4096], P('dp', None, 'tensor'), as said below
- fresh_keys: bfloat16 [4, 512, 4096], P(None, 'dp', 'tensor'), as said below
- fresh_values: bfloat16 [4, 512, 4096], P(None, 'dp', 'tensor'), as said below
- lengths: int32 [512], P('dp'), may hold values from 1 to 128, as said below
Outputs:
- decoded: bfloat16 [4, 512, 8192], P(None, 'dp', 'tensor')
- stepped_down: float32 [8192, 64], P('tensor')
- stepped_up: float32 [64, 8192], P(None, 'tensor')
- stepped_down_first: float32 [8192, 64], P('tensor')
- stepped_down_second: float32 [8192, 64], P('tensor')
- stepped_up_first: float32 [64, 8192], P(None, 'tensor')
- stepped_up_second: float32 [64, 8192], P(None, 'tensor')
Inputs may be any that keep to these rules, and one draw needn't show every extreme that they name: `lengths`: the largest length is 128 in every draw. `stored_keys`: 8 key heads of size 128; features t * 128 to (t+1) * 128 - 1 hold head t // (32 / 8), so each head stands at 32 / 8 neighbouring tensor indices. `stored_values`: 8 value heads, laid out as stored_keys. `fresh_keys`: 8 key heads, laid out as stored_keys. `fresh_values`: 8 value heads, laid out as stored_keys.
All inputs are finite; a program needn't handle non-finite values.
Results may differ from a plain program's by a relative error of at most 0.0057.
Values sent between devices are 32-bit elements; how exact they have to be, the bound alone decides.
A program may use at most 64 MiB of HBM per device.

v0:
```python
import math

import jax
import jax.numpy as jnp
from jax import lax
from jax.sharding import PartitionSpec as P

beta_one = 0.9
beta_two = 0.999
learn_rate = 0.005
adam_count = 10.0
adam_eps = 1e-08
adapter_scale = 2.0


def apply_adam_step(current, moment_one, moment_two, gradient):
    moment_one = beta_one * moment_one + (1.0 - beta_one) * gradient
    moment_two = beta_two * moment_two + (1.0 - beta_two) * gradient * gradient
    fix_one = 1.0 - beta_one**adam_count
    fix_two = 1.0 - beta_two**adam_count
    updated = current - learn_rate * (moment_one / fix_one) / (
        jnp.sqrt(moment_two / fix_two) + adam_eps
    )
    return (updated, moment_one, moment_two)


def attend(queries, stored_keys, stored_values, fresh_keys, fresh_values, lengths):
    num_steps, num_rows, features = queries.shape
    head_size = stored_keys.shape[2]
    group_size = features // head_size
    inv_root = 1.0 / math.sqrt(head_size)
    query_heads = queries.reshape(num_steps, num_rows, group_size, head_size)
    score_cache = (
        jnp.einsum("srgd,rcd->srgc", query_heads, stored_keys, preferred_element_type=jnp.float32)
        * inv_root
    )
    score_new = (
        jnp.einsum("srgd,jrd->srgj", query_heads, fresh_keys, preferred_element_type=jnp.float32)
        * inv_root
    )
    cache_live = (jnp.arange(stored_keys.shape[1])[None, :] < lengths[:, None])[None, :, None, :]
    new_live = (jnp.arange(num_steps)[None, :] <= jnp.arange(num_steps)[:, None])[:, None, None, :]
    score_cache = jnp.where(cache_live, score_cache, -1e30)
    score_new = jnp.where(new_live, score_new, -1e30)
    largest = jnp.maximum(jnp.max(score_cache, axis=-1), jnp.max(score_new, axis=-1))[..., None]
    exp_cache = jnp.where(cache_live, jnp.exp(score_cache - largest), 0.0)
    exp_new = jnp.where(new_live, jnp.exp(score_new - largest), 0.0)
    total = (jnp.sum(exp_cache, axis=-1) + jnp.sum(exp_new, axis=-1))[..., None]
    weight_cache = (exp_cache / total).astype(jnp.bfloat16)
    weight_new = (exp_new / total).astype(jnp.bfloat16)
    mixed = jnp.einsum(
        "srgc,rcd->srgd", weight_cache, stored_values, preferred_element_type=jnp.float32
    )
    mixed = mixed + jnp.einsum(
        "srgj,jrd->srgd", weight_new, fresh_values, preferred_element_type=jnp.float32
    )
    return mixed.reshape(num_steps * num_rows, features).astype(jnp.bfloat16)


def per_device(
    projection_input,
    output_gradient,
    adapter_down,
    adapter_up,
    down_first_moment,
    down_second_moment,
    up_first_moment,
    up_second_moment,
    projection_weight,
    queries,
    stored_keys,
    stored_values,
    fresh_keys,
    fresh_values,
    lengths,
):
    highest_precision = lax.Precision.HIGHEST
    input_wide_float = projection_input.astype(jnp.float32)
    gradient_wide_float = output_gradient.astype(jnp.float32)
    input_slice = jnp.dot(input_wide_float, adapter_down, precision=highest_precision)
    gradient_slice = jnp.dot(gradient_wide_float, adapter_up.T, precision=highest_precision)
    input_times_down, gradient_through_up = lax.psum((input_slice, gradient_slice), "tensor")
    token_total = projection_input.shape[0] * lax.axis_size("dp")
    scale_coefficient = adapter_scale / token_total
    down_gradient = scale_coefficient * jnp.dot(
        input_wide_float.T, gradient_through_up, precision=highest_precision
    )
    up_gradient = scale_coefficient * jnp.dot(
        input_times_down.T, gradient_wide_float, precision=highest_precision
    )
    down_gradient, up_gradient = lax.psum((down_gradient, up_gradient), "dp")
    stepped_down, stepped_down_first, stepped_down_second = apply_adam_step(
        adapter_down, down_first_moment, down_second_moment, down_gradient
    )
    stepped_up, stepped_up_first, stepped_up_second = apply_adam_step(
        adapter_up, up_first_moment, up_second_moment, up_gradient
    )
    attention_output = attend(
        queries, stored_keys, stored_values, fresh_keys, fresh_values, lengths
    )
    num_steps, num_rows = (queries.shape[0], queries.shape[1])
    whole_b = lax.all_gather(stepped_up, "tensor", axis=1, tiled=True)
    combined_weight = projection_weight.astype(jnp.float32) + adapter_scale * jnp.dot(
        stepped_down, whole_b, precision=highest_precision
    )
    partial_value = jnp.dot(
        attention_output.astype(jnp.float32), combined_weight, precision=highest_precision
    )
    summed = lax.psum_scatter(partial_value, "tensor", scatter_dimension=1, tiled=True)
    decoded = summed.reshape(num_steps, num_rows, summed.shape[1]).astype(jnp.bfloat16)
    return (
        decoded,
        stepped_down,
        stepped_up,
        stepped_down_first,
        stepped_down_second,
        stepped_up_first,
        stepped_up_second,
    )


def solution(mesh):
    return jax.shard_map(
        per_device,
        mesh=mesh,
        in_specs=(
            P("dp", "tensor"),
            P("dp", "tensor"),
            P("tensor", None),
            P(None, "tensor"),
            P("tensor", None),
            P("tensor", None),
            P(None, "tensor"),
            P(None, "tensor"),
            P("tensor", None),
            P(None, "dp", "tensor"),
            P("dp", None, "tensor"),
            P("dp", None, "tensor"),
            P(None, "dp", "tensor"),
            P(None, "dp", "tensor"),
            P("dp"),
        ),
        out_specs=(
            P(None, "dp", "tensor"),
            P("tensor", None),
            P(None, "tensor"),
            P("tensor", None),
            P("tensor", None),
            P(None, "tensor"),
            P(None, "tensor"),
        ),
        check_vma=False,
    )
```

profile of v0, /device:TPU:1, one launch (start us, length us, event | category | flops | bytes accessed | tf_op | source)
XLA Modules:
  0.0 525.7 jit_solution(1403165785465469162)
XLA Ops:
  7.2 0.0 copy-start
  7.2 0.0 copy-start.3
  7.2 0.0 all-reduce.5.cloned.1.call-start
  7.2 2.0 fusion.47
  9.2 1.8 fusion.46
  11.0 0.0 all-reduce.5.cloned.1.call-update
  11.0 0.0 all-reduce.7.cloned.1.call-start
  11.1 205.8 %all-reduce.5.cloned.1.call-done = (f32[256,64]{0,1:T(8,128)}, f32[256,64]{0,1:T(8,128)}) async-done(((f32[256,64]{0,1:T(8,128)}, f32[256,64]{0,1:T(8,128)}), (f32[256,64]{0,1:T(8,128)}, f32[256,64]{0,1:T(8,128)})) %all-reduce.5.cloned.1.call-update) | async-done | bytes 131088 | tf_op jit(solution)/shard_map/psum | solution.py:82
  216.8 1.8 fusion.23
  218.6 1.8 convolution_multiply_fusion.1
  220.4 0.0 all-reduce.7.cloned.1.call-update
  220.4 0.0 all-gather.2.cloned.1.call-start
  220.5 83.8 %all-reduce.7.cloned.1.call-done = (f32[256,64]{0,1:T(8,128)}, f32[64,256]{1,0:T(8,128)}) async-done(((f32[256,64]{0,1:T(8,128)}, f32[64,256]{1,0:T(8,128)}), (f32[256,64]{0,1:T(8,128)}, f32[64,256]{1,0:T(8,128)})) %all-reduce.7.cloned.1.call-update) | async-done | bytes 131088 | tf_op jit(solution)/shard_map/psum | solution.py:91
  304.3 1.6 divide_subtract_fusion
  306.0 0.0 all-gather.2.cloned.1.call-update
  306.0 0.0 reduce-scatter.2.cloned.1.call-start
  306.0 0.9 reshape.60
  307.0 1.1 fusion.33
  308.1 0.1 copy.54
  308.3 0.1 fusion.40
  308.4 0.1 copy.55
  308.5 0.7 iota_compare_fusion
  309.2 0.0 copy-done
  309.2 1.3 fusion.45
  310.6 0.1 copy.56
  310.7 0.1 fusion.41
  310.8 0.1 copy.57
  310.9 0.4 fusion.24
  311.4 0.1 copy.58
  311.5 0.1 divide_convert_fusion.2
  311.6 0.2 copy.59
  311.8 0.0 copy-done.3
  311.8 0.2 fusion.37
  312.0 0.0 copy-start.2
  312.0 0.0 copy-start.4
  312.0 0.0 copy-start.5
  312.0 0.0 copy-start.6
  312.0 2.4 fusion.20
  314.4 0.1 copy.61
  314.6 0.0 copy-done.2
  314.6 0.0 copy-done.4
  314.6 0.0 copy-done.5
  314.6 0.0 copy-done.6
  314.6 0.7 divide_subtract_fusion.1
  315.3 0.0 copy-start.1
  315.3 59.6 %all-gather.2.cloned.1.call-done = f32[64,8192]{1,0:T(8,128)} async-done(((f32[64,256]{1,0:T(8,128)}), f32[64,8192]{1,0:T(8,128)}) %all-gather.2.cloned.1.call-update) | async-done | bytes 2097168 | tf_op jit(solution)/shard_map/all_gather | solution.py:102
  374.9 9.4 %fusion = f32[256,8192]{1,0:T(8,128)S(1)} fusion(f32[256,64]{0,1:T(8,128)S(1)} %get-tuple-element.14, f32[64,8192]{1,0:T(8,128)} %all-gather.2.cloned.1.call-done, bf16[256,8192]{1,0:T(8,128)(2,1)} %param.23), kind=kOutput, calls=%fused_computation.1 | convolution fusion | flops 1616904192 | bytes 14745600 | tf_op jit(solution)/shard_map/dot_general | solution.py:103
  384.3 0.0 copy-done.1
  384.3 6.7 %fusion.25 = f32[256,8192]{1,0:T(8,128)} fusion(f32[256,8192]{1,0:T(8,128)S(1)} %fusion, bf16[32,8,2,128]{3,2,1,0:T(2,128)(2,1)S(1)} %bitcast.60), kind=kOutput, calls=%fused_computation.18 | convolution fusion | flops 6442450944 | bytes 16908288 | tf_op jit(solution)/shard_map/dot_general | solution.py:106
  391.0 0.0 reduce-scatter.2.cloned.1.call-update
  391.0 126.5 %reduce-scatter.2.cloned.1.call-done = f32[256,256]{1,0:T(8,128)} async-done(((f32[256,8192]{1,0:T(8,128)}), f32[256,256]{1,0:T(8,128)}) %reduce-scatter.2.cloned.1.call-update) | async-done | bytes 262160 | tf_op jit(solution)/shard_map/reduce_scatter | solution.py:109
  517.5 1.6 convert_element_type.33
  (3 shorter events, 0.1 us)
Async XLA Ops:
  7.2 302.1 %copy-start = (bf16[64,128,128]{2,1,0:T(8,128)(2,1)S(1)}, bf16[64,128,128]{2,1,0:T(8,128)(2,1)}, u32[]{:S(2)}) copy-start(bf16[64,128,128]{2,1,0:T(8,128)(2,1)} %param.25) | copy-start | bytes 6291460
  7.2 304.6 %copy-start.3 = (bf16[4,64,128]{2,1,0:T(8,128)(2,1)S(1)}, bf16[4,64,128]{2,1,0:T(8,128)(2,1)}, u32[]{:S(2)}) copy-start(bf16[4,64,128]{2,1,0:T(8,128)(2,1)} %param.28) | copy-start | bytes 196612
  7.2 209.7 %all-reduce.5.cloned.1.call-start = ((), (), s32[]{:S(2)}) async-start(), calls=%async_computation.3 | async-start | bytes 262144 | tf_op jit(solution)/shard_map/psum | solution.py:82
  11.0 293.3 %all-reduce.7.cloned.1.call-start = ((), (), s32[]{:S(2)}) async-start(), calls=%async_computation.4 | async-start | bytes 262144 | tf_op jit(solution)/shard_map/psum | solution.py:91
  220.4 154.5 %all-gather.2.cloned.1.call-start = ((), (), s32[]{:S(2)}) async-start(), calls=%async_computation.1 | async-start | bytes 2162688 | tf_op jit(solution)/shard_map/all_gather | solution.py:102
  306.0 211.5 %reduce-scatter.2.cloned.1.call-start = ((), (), s32[]{:S(2)}) async-start(), calls=%async_computation.2 | async-start | bytes 8650752 | tf_op jit(solution)/shard_map/reduce_scatter | solution.py:109
  312.0 2.6 copy-start.2
  312.0 2.6 copy-start.4
  312.0 2.6 copy-start.5
  312.0 2.6 copy-start.6
  315.3 69.0 %copy-start.1 = (f32[256,64]{0,1:T(8,128)}, f32[256,64]{0,1:T(8,128)S(1)}, u32[]{:S(2)}) copy-start(f32[256,64]{0,1:T(8,128)S(1)} %get-tuple-element.14) | copy-start | bytes 196612
Sparse Core Ops, SparseCore 0:
  11.3 205.5 all-reduce.4
  220.6 83.7 all-reduce.6
  306.8 68.0 all-gather.1
  391.1 126.3 reduce-scatter.1
where the time goes:
time: 529 us; the launch traced here: 526 us
  waiting for transfers between devices  476 us (90%)
  matrix products  28.4 us (5%)
  between operations  14 us (3%)
  other arithmetic  5.5 us (1%)
    psum x1, waiting for transfers between devices, per_device(): lax.psum((input_slice, gradient_slice), 'tensor')  206 us
    reduce_scatter x1, waiting for transfers between devices, per_device(): lax.psum_scatter(partial_value, 'tensor', scatter_dimension=1, tiled=True)  127 us
    psum x1, waiting for transfers between devices, per_device(): down_gradient, up_gradient = lax.psum((down_gradient, up_gradient), 'dp')  83.8 us
    all_gather x1, waiting for transfers between devices, per_device(): whole_b = lax.all_gather(stepped_up, 'tensor', axis=1, tiled=True)  59.6 us
  transfers between devices with their start and end apart: 4, of which 4 were waited for; matrix products, arithmetic and copies ran while one was open for 2% of the time, Pallas kernels for 0%

commit v1 on v0

v1 whole, which is shorter than its diff:
```python
import functools
import math

import jax
import jax.numpy as jnp
from jax import lax
from jax.experimental import pallas as pl
from jax.experimental.pallas import tpu as pltpu
from jax.sharding import PartitionSpec as P

beta_one = 0.9
beta_two = 0.999
learn_rate = 0.005
adam_count = 10.0
adam_eps = 1e-08
adapter_scale = 2.0

F32 = jnp.float32
BF16 = jnp.bfloat16
MESH = pl.DeviceIdType.MESH

ROWS = 256
FEAT = 256
RANK = 64
ZN = 8
DP = 8
HALF = ROWS // 2
ROWS_A = 64
ROWS_B = HALF - ROWS_A


def apply_adam_step(current, moment_one, moment_two, gradient):
    moment_one = beta_one * moment_one + (1.0 - beta_one) * gradient
    moment_two = beta_two * moment_two + (1.0 - beta_two) * gradient * gradient
    fix_one = 1.0 - beta_one**adam_count
    fix_two = 1.0 - beta_two**adam_count
    updated = current - learn_rate * (moment_one / fix_one) / (
        jnp.sqrt(moment_two / fix_two) + adam_eps
    )
    return (updated, moment_one, moment_two)


def dot(a, b):
    return jnp.dot(a, b, preferred_element_type=F32)


def dot_t(a, b):
    return lax.dot_general(a, b, (((1,), (1,)), ((), ())), preferred_element_type=F32)


def two_terms(a):
    high = a.astype(BF16)
    low = (a - high.astype(F32)).astype(BF16)
    return high, low


def attention_kernel(
    len_ref, q_ref, k_ref, v_ref, fk_ref, fv_ref, out_ref, qs, sc, sn, wc, mixed
):
    pairs = k_ref.shape[0] // 2
    inv_root = 1.0 / math.sqrt(128)
    i0 = lax.broadcasted_iota(jnp.int32, (ROWS, ROWS), 0)
    i1 = lax.broadcasted_iota(jnp.int32, (ROWS, ROWS), 1)
    perm = jnp.where(i1 == (i0 % 4) * 64 + i0 // 4, 1.0, 0.0).astype(BF16)
    qp = dot(perm, q_ref[...])
    qp = jnp.concatenate(
        [qp[:, :128].reshape(pairs, 8, 128), qp[:, 128:].reshape(pairs, 8, 128)], axis=1
    )
    qs[...] = qp.reshape(pairs * 16, 128).astype(BF16)
    fk = dot(perm, fk_ref[...]).astype(BF16)
    fv = dot(perm, fv_ref[...]).astype(BF16)

    row = lax.broadcasted_iota(jnp.int32, (16, 256), 0)
    col = lax.broadcasted_iota(jnp.int32, (16, 256), 1)
    second = (row // 4) % 2 == 1

    def scores(p, carry):
        keys = k_ref[pl.ds(2 * p, 2)].reshape(256, 128)
        at = pl.ds(pl.multiple_of(p * 16, 16), 16)
        s = dot_t(qs[at, :], keys) * inv_root
        start = jnp.where(second, 128, 0)
        stop = jnp.where(second, 128 + len_ref[2 * p + 1], len_ref[2 * p])
        sc[at, :] = jnp.where((col >= start) & (col < stop), s, -jnp.inf)
        return carry

    lax.fori_loop(0, pairs, scores, 0, unroll=8)

    nrow = lax.broadcasted_iota(jnp.int32, (256, 128), 0)
    ncol = lax.broadcasted_iota(jnp.int32, (256, 128), 1)
    request = (nrow // 16) * 2 + (nrow // 4) % 2
    new_live = (ncol // 4 == request) & (ncol % 4 <= nrow % 4)
    for half in range(2):
        part = pl.ds(half * 256, 256)
        s = dot_t(qs[part, :], fk[half * 128 : half * 128 + 128]) * inv_root
        sn[part, :] = jnp.where(new_live, s, -jnp.inf)

    for block in range(8):
        part = pl.ds(block * 64, 64)
        s, n = sc[part, :], sn[part, :]
        largest = jnp.maximum(
            jnp.max(s, axis=1, keepdims=True), jnp.max(n, axis=1, keepdims=True)
        )
        e, m = jnp.exp(s - largest), jnp.exp(n - largest)
        total = jnp.sum(e, axis=1, keepdims=True) + jnp.sum(m, axis=1, keepdims=True)
        scale = 1.0 / total
        wc[part, :] = (e * scale).astype(BF16)
        where_new = (block // 4) * 128
        mixed[part, :] = dot((m * scale).astype(BF16), fv[where_new : where_new + 128])

    def mix(p, carry):
        values = v_ref[pl.ds(2 * p, 2)].reshape(256, 128)
        at = pl.ds(pl.multiple_of(p * 16, 16), 16)
        mixed[at, :] += dot(wc[at, :], values)
        return carry

    lax.fori_loop(0, pairs, mix, 0, unroll=8)
    o = mixed[...].reshape(pairs, 16, 128)
    out_ref[:, :128] = o[:, :8].reshape(ROWS, 128).astype(BF16)
    out_ref[:, 128:] = o[:, 8:].reshape(ROWS, 128).astype(BF16)


def attention(lengths, queries, keys, values, fresh_keys, fresh_values):
    vmem = pl.BlockSpec(memory_space=pltpu.VMEM)
    return pl.pallas_call(
        attention_kernel,
        out_shape=jax.ShapeDtypeStruct((ROWS, FEAT), BF16),
        in_specs=[pl.BlockSpec(memory_space=pltpu.SMEM)] + [vmem] * 5,
        out_specs=vmem,
        scratch_shapes=[
            pltpu.VMEM((512, 128), BF16),
            pltpu.VMEM((512, 256), F32),
            pltpu.VMEM((512, 128), F32),
            pltpu.VMEM((512, 256), BF16),
            pltpu.VMEM((512, 128), F32),
        ],
        compiler_params=pltpu.CompilerParams(vmem_limit_bytes=24 * 1024 * 1024),
    )(lengths, queries, keys, values, fresh_keys, fresh_values)


def step_kernel(
    attn, x, dy, a_ref, b_ref, am_ref, av_ref, bm_ref, bv_ref, w_hbm,
    dec, a_out, b_out, am_out, av_out, bm_out, bv_out,
    w, csend, crecv, ysend, yrecv, zsa, zra, zsb, zrb, yfin,
    one_in, one_z, one_g, one_gr, one_out,
    grad, grad_r, grad_out,
    two_in, two_z, two_g, two_gr, two_out,
    w_sem, c_s, c_r, y_s, y_r, za_s, za_r, zb_s, zb_r, yf_s, yf_r, t_s, t_r,
):
    d = lax.axis_index("dp")
    t = lax.axis_index("tensor")
    z, y, c = t // 4, (t // 2) % 2, t % 2

    def at(zz, yy, cc):
        return (d, (zz * 2 + yy) * 2 + cc)

    core_peer = at(z, y, 1 - c)
    y_peer = at(z, 1 - y, c)
    z_peers = [at(lax.rem(z + k, ZN), y, c) for k in range(1, ZN)]
    group = [core_peer, y_peer, at(z, 1 - y, 1 - c)]
    dp_peers = [(lax.rem(d + k, DP), t) for k in range(1, DP)]

    load_w = pltpu.make_async_copy(w_hbm, w, w_sem)
    load_w.start()

    barrier = pltpu.get_barrier_semaphore()
    everyone = z_peers + group + dp_peers
    for peer in everyone:
        pl.semaphore_signal(barrier, inc=1, device_id=peer, device_id_type=MESH)

    def remote(src, dst, send_sem, recv_sem, peer):
        return pltpu.make_async_remote_copy(
            src_ref=src,
            dst_ref=dst,
            send_sem=send_sem,
            recv_sem=recv_sem,
            device_id=peer,
            device_id_type=MESH,
        )

    class TensorSum:
        def __init__(self, src, z_recv, mine, g_recv, out, first):
            self.src, self.z_recv, self.mine = src, z_recv, mine
            self.g_recv, self.out, self.first = g_recv, out, first
            self.here = pl.ds(pl.multiple_of(z * 32, 32), 32)

        def scatter(self, k):
            part = pl.ds(pl.multiple_of(lax.rem(z + k, ZN) * 32, 32), 32)
            i = self.first + k - 1
            return remote(
                self.src.at[part], self.z_recv.at[k - 1], t_s.at[i], t_r.at[i], z_peers[k - 1]
            )

        def exchange(self, m):
            i = self.first + 7 + m
            return remote(self.mine, self.g_recv.at[m], t_s.at[i], t_r.at[i], group[m])

        def gather(self, k):
            i = self.first + 10 + k - 1
            return remote(
                self.out.at[self.here], self.out.at[self.here], t_s.at[i], t_r.at[i], z_peers[k - 1]
            )

        def one(self):
            for k in range(1, ZN):
                self.scatter(k).start()

        def two(self):
            for k in range(1, ZN):
                self.scatter(k).wait_recv()
            total = self.src[self.here, :]
            for k in range(1, ZN):
                total = total + self.z_recv[k - 1]
            self.mine[...] = total
            for m in range(3):
                self.exchange(m).start()

        def three(self):
            for m in range(3):
                self.exchange(m).wait_recv()
            self.out[self.here, :] = (self.mine[...] + self.g_recv[0]) + (
                self.g_recv[1] + self.g_recv[2]
            )
            for k in range(1, ZN):
                self.gather(k).start()

        def four(self):
            for k in range(1, ZN):
                self.gather(k).wait_recv()

        def finish(self):
            for k in range(1, ZN):
                self.scatter(k).wait_send()
                self.gather(k).wait_send()
            for m in range(3):
                self.exchange(m).wait_send()

    sum_one = TensorSum(one_in, one_z, one_g, one_gr, one_out, 0)
    sum_two = TensorSum(two_in, two_z, two_g, two_gr, two_out, 17)

    a_high, a_low = two_terms(a_ref[...])
    b_high, b_low = two_terms(b_ref[...])
    one_in[...] = jnp.concatenate(
        [
            dot(x[...], a_high) + dot(x[...], a_low),
            dot_t(dy[...], b_high) + dot_t(dy[...], b_low),
        ],
        axis=1,
    )
    pl.semaphore_wait(barrier, len(everyone))
    sum_one.one()

    d_here = pl.ds(pl.multiple_of(d * 16, 16), 16)

    def grad_scatter(k):
        part = pl.ds(pl.multiple_of(lax.rem(d + k, DP) * 16, 16), 16)
        i = 34 + k - 1
        return remote(grad.at[part], grad_r.at[k - 1], t_s.at[i], t_r.at[i], dp_peers[k - 1])

    def grad_gather(k):
        i = 41 + k - 1
        return remote(
            grad_out.at[d_here], grad_out.at[d_here], t_s.at[i], t_r.at[i], dp_peers[k - 1]
        )

    def gradients():
        sum_one.four()
        scale = adapter_scale / (ROWS * DP)
        both = one_out[...].T
        x_high, x_low = two_terms(both[:RANK])
        g_high, g_low = two_terms(both[RANK:])
        grad[:RANK, :] = scale * (dot(g_high, x[...]) + dot(g_low, x[...]))
        grad[RANK:, :] = scale * (dot(x_high, dy[...]) + dot(x_low, dy[...]))
        for k in range(1, DP):
            grad_scatter(k).start()

    def gradient_sum():
        for k in range(1, DP):
            grad_scatter(k).wait_recv()
        total = grad[d_here, :]
        for k in range(1, DP):
            total = total + grad_r[k - 1]
        grad_out[d_here, :] = total
        for k in range(1, DP):
            grad_gather(k).start()

    def update():
        for k in range(1, DP):
            grad_gather(k).wait_recv()
        new_a, a_one, a_two = apply_adam_step(
            a_ref[...], am_ref[...], av_ref[...], grad_out[:RANK, :].T
        )
        a_out[...], am_out[...], av_out[...] = new_a, a_one, a_two
        new_b, b_one, b_two = apply_adam_step(
            b_ref[...], bm_ref[...], bv_ref[...], grad_out[RANK:, :]
        )
        b_out[...], bm_out[...], bv_out[...] = new_b, b_one, b_two
        high, low = two_terms(new_a)
        two_in[...] = dot(attn[...], jnp.concatenate([high, low], axis=1))
        sum_two.one()

    up, down = lax.rem(z + 1, ZN), lax.rem(z + ZN - 1, ZN)
    sides = [at(up, y, c), at(down, y, c)]

    def destination(step, side):
        return lax.rem(z + 2 * ZN - 1 - step, ZN) if side == 0 else lax.rem(z + 1 + step, ZN)

    def product(step, side, other_y, other_c):
        yy = (1 - y) if other_y else y
        cc = (1 - c) if other_c else c
        block = (destination(step, side) * 2 + yy) * 2 + cc
        cols = pl.ds(pl.multiple_of(block * FEAT, FEAT), FEAT)
        return dot(attn[pl.ds(side * HALF, HALF), :], w[:, cols])

    def core_copy(step, side):
        return remote(
            csend.at[step, side], crecv.at[step, side],
            c_s.at[step, side], c_r.at[step, side], core_peer,
        )

    def y_copy(step, side):
        return remote(
            ysend.at[step, side], yrecv.at[step, side],
            y_s.at[step, side], y_r.at[step, side], y_peer,
        )

    def za_copy(step, side):
        return remote(
            zsa.at[step, side], zra.at[step, side],
            za_s.at[step, side], za_r.at[step, side], sides[side],
        )

    def zb_copy(step, side):
        return remote(
            zsb.at[step, side], zrb.at[step, side],
            zb_s.at[step, side], zb_r.at[step, side], sides[side],
        )

    def yfin_copy(side):
        return remote(
            zsa.at[ZN - 1, side, 1], yfin.at[side], yf_s.at[side], yf_r.at[side], y_peer
        )

    def core_stage(step):
        for side in range(2):
            for k in range(2):
                csend[step, side, k] = product(step, side, k == 1, True)
            core_copy(step, side).start()

    def y_stage(step):
        for side in range(2):
            own = product(step, side, False, False)
            other = product(step, side, True, False)
            core_copy(step, side).wait_recv()
            own = own + crecv[step, side, 0]
            other = other + crecv[step, side, 1]
            ysend[step, side] = other[ROWS_A:]
            y_copy(step, side).start()
            zsa[step, side, 0] = own[:ROWS_A]
            zsa[step, side, 1] = other[:ROWS_A]
            zsb[step, side] = own[ROWS_A:]

    def z_stage(step):
        for side in range(2):
            @pl.when(step > 0)
            def _():
                za_copy(step - 1, side).wait_recv()
                zsa[step, side] += zra[step - 1, side]

            @pl.when(step < ZN - 1)
            def _():
                za_copy(step, side).start()

        for side in range(2):
            y_copy(step, side).wait_recv()

            @pl.when(step > 0)
            def _():
                zb_copy(step - 1, side).wait_recv()
                zsb[step, side] += zrb[step - 1, side] + yrecv[step, side]

            @pl.when(step == 0)
            def _():
                zsb[step, side] += yrecv[step, side]

            @pl.when(step < ZN - 1)
            def _():
                zb_copy(step, side).start()

    load_w.wait()
    core_stage(0)
    core_stage(1)
    y_stage(0)
    sum_one.two()

    at_step = {
        0: sum_one.three,
        1: gradients,
        2: gradient_sum,
        3: update,
        4: sum_two.two,
        5: sum_two.three,
    }

    def ring(step, carry):
        z_stage(step)

        @pl.when(step < ZN - 1)
        def _():
            y_stage(step + 1)

        @pl.when(step < ZN - 2)
        def _():
            core_stage(step + 2)

        for when, work in at_step.items():
            pl.when(step == when)(work)
        return carry

    lax.fori_loop(0, ZN, ring, 0)
    for side in range(2):
        yfin_copy(side).start()

    sum_two.four()
    u_high, u_low = two_terms(two_out[...])
    b_high, b_low = two_terms(b_out[...])
    left = jnp.concatenate([u_high, u_low, u_high], axis=1)
    right = jnp.concatenate([b_high, b_high, b_high, b_high, b_low, b_low], axis=0)
    delta = adapter_scale * dot(left, right)

    for side in range(2):
        rows_b = pl.ds(side * HALF + ROWS_A, ROWS_B)
        dec[rows_b, :] = (
            zsb[ZN - 1, side] + delta[side * HALF + ROWS_A : (side + 1) * HALF]
        ).astype(BF16)
    for side in range(2):
        yfin_copy(side).wait_recv()
        rows_a = pl.ds(side * HALF, ROWS_A)
        dec[rows_a, :] = (
            (zsa[ZN - 1, side, 0] + yfin[side]) + delta[side * HALF : side * HALF + ROWS_A]
        ).astype(BF16)

    sum_one.finish()
    sum_two.finish()
    for k in range(1, DP):
        grad_scatter(k).wait_send()
        grad_gather(k).wait_send()
    for side in range(2):
        yfin_copy(side).wait_send()

    def drain(step, carry):
        for side in range(2):
            core_copy(step, side).wait_send()
            y_copy(step, side).wait_send()

            @pl.when(step < ZN - 1)
            def _():
                za_copy(step, side).wait_send()
                zb_copy(step, side).wait_send()

        return carry

    lax.fori_loop(0, ZN, drain, 0)


def step(attn, x, dy, a, b, am, av, bm, bv, weight):
    vmem = pl.BlockSpec(memory_space=pltpu.VMEM)
    down = jax.ShapeDtypeStruct((FEAT, RANK), F32)
    up = jax.ShapeDtypeStruct((RANK, FEAT), F32)
    dma = pltpu.SemaphoreType.DMA
    small = [
        pltpu.VMEM((256, 128), F32),
        pltpu.VMEM((7, 32, 128), F32),
        pltpu.VMEM((32, 128), F32),
        pltpu.VMEM((3, 32, 128), F32),
        pltpu.VMEM((256, 128), F32),
    ]
    return pl.pallas_call(
        step_kernel,
        out_shape=(
            jax.ShapeDtypeStruct((ROWS, FEAT), BF16), down, up, down, down, up, up
        ),
        in_specs=[vmem] * 9 + [pl.BlockSpec(memory_space=pl.ANY)],
        out_specs=(vmem,) * 7,
        scratch_shapes=[
            pltpu.VMEM((FEAT, 8192), BF16),
            pltpu.VMEM((ZN, 2, 2, HALF, FEAT), F32),
            pltpu.VMEM((ZN, 2, 2, HALF, FEAT), F32),
            pltpu.VMEM((ZN, 2, ROWS_B, FEAT), F32),
            pltpu.VMEM((ZN, 2, ROWS_B, FEAT), F32),
            pltpu.VMEM((ZN, 2, 2, ROWS_A, FEAT), F32),
            pltpu.VMEM((ZN - 1, 2, 2, ROWS_A, FEAT), F32),
            pltpu.VMEM((ZN, 2, ROWS_B, FEAT), F32),
            pltpu.VMEM((ZN - 1, 2, ROWS_B, FEAT), F32),
            pltpu.VMEM((2, ROWS_A, FEAT), F32),
            *small,
            pltpu.VMEM((128, FEAT), F32),
            pltpu.VMEM((7, 16, FEAT), F32),
            pltpu.VMEM((128, FEAT), F32),
            *small,
            dma,
            dma((ZN, 2)), dma((ZN, 2)), dma((ZN, 2)), dma((ZN, 2)),
            dma((ZN - 1, 2)), dma((ZN - 1, 2)), dma((ZN - 1, 2)), dma((ZN - 1, 2)),
            dma((2,)), dma((2,)),
            dma((48,)), dma((48,)),
        ],
        compiler_params=pltpu.CompilerParams(
            collective_id=0, has_side_effects=True, vmem_limit_bytes=40 * 1024 * 1024
        ),
    )(attn, x, dy, a, b, am, av, bm, bv, weight)


def per_device(
    projection_input,
    output_gradient,
    adapter_down,
    adapter_up,
    down_first_moment,
    down_second_moment,
    up_first_moment,
    up_second_moment,
    projection_weight,
    queries,
    stored_keys,
    stored_values,
    fresh_keys,
    fresh_values,
    lengths,
):
    attn = attention(
        lengths,
        queries.reshape(ROWS, FEAT),
        stored_keys,
        stored_values,
        fresh_keys.reshape(ROWS, 128),
        fresh_values.reshape(ROWS, 128),
    )
    decoded, *rest = step(
        attn,
        projection_input,
        output_gradient,
        adapter_down,
        adapter_up,
        down_first_moment,
        down_second_moment,
        up_first_moment,
        up_second_moment,
        projection_weight,
    )
    decoded = decoded.reshape(64, 4, FEAT).transpose(1, 0, 2)
    new_a, new_b, a_one, a_two, b_one, b_two = rest
    return (decoded, new_a, new_b, a_one, a_two, b_one, b_two)


def solution(mesh):
    return jax.shard_map(
        per_device,
        mesh=mesh,
        in_specs=(
            P("dp", "tensor"),
            P("dp", "tensor"),
            P("tensor", None),
            P(None, "tensor"),
            P("tensor", None),
            P("tensor", None),
            P(None, "tensor"),
            P(None, "tensor"),
            P("tensor", None),
            P(None, "dp", "tensor"),
            P("dp", None, "tensor"),
            P("dp", None, "tensor"),
            P(None, "dp", "tensor"),
            P(None, "dp", "tensor"),
            P("dp"),
        ),
        out_specs=(
            P(None, "dp", "tensor"),
            P("tensor", None),
            P(None, "tensor"),
            P("tensor", None),
            P("tensor", None),
            P(None, "tensor"),
            P(None, "tensor"),
        ),
        check_vma=False,
    )
```

time: 529 us -> 80.5 us (0.15)
  the two profiles are of different devices: /device:TPU:1 before, /device:TPU:72 now
where the time goes in v1:
time: 80.5 us; the launch traced here: 80.1 us
  Pallas kernels  65.4 us (81%)
  local copies, waits for them, and re-layouts  14 us (17%)
    pallas_call x1, Pallas kernels, step(): pl.pallas_call(step_kernel, out_shape=(jax.ShapeDtypeStruct((ROWS, FEAT),...  62.2 us
    unnamed x33, local copies, waits for them, and re-layouts  13.3 us
    pallas_call x1, Pallas kernels, attention(): pl.pallas_call(attention_kernel, out_shape=jax.ShapeDtypeStruct((ROWS, FE...  3.17 us

profile of v1, /device:TPU:72, one launch (start us, length us, event | category | flops | bytes accessed | tf_op | source)
XLA Modules:
  0.0 80.1 jit_solution(163066575262253143)
XLA Ops:
  0.6 0.9 %copy.22.a_ref = f32[256,64]{1,0:T(8,128)S(1)} copy(f32[256,64]{0,1:T(8,128)} %param.17) | data formatting | bytes 131072 | tf_op args[2]
  1.6 0.9 %copy.23.am_ref = f32[256,64]{1,0:T(8,128)S(1)} copy(f32[256,64]{0,1:T(8,128)} %param.19) | data formatting | bytes 131072 | tf_op args[4]
  2.5 0.0 copy-start.10
  2.5 1.0 %copy.24.av_ref = f32[256,64]{1,0:T(8,128)S(1)} copy(f32[256,64]{0,1:T(8,128)} %param.20) | data formatting | bytes 131072 | tf_op args[5]
  3.5 0.0 copy-start.1
  3.5 1.6 %copy-done.1 = bf16[64,128,128]{2,1,0:T(8,128)(2,1)S(1)} copy-done((bf16[64,128,128]{2,1,0:T(8,128)(2,1)S(1)}, bf16[64,128,128]{2,1,0:T(8,128)(2,1)}, u32[]{:S(2)}) %copy-start.1) | copy-done | bytes 2097176
  5.1 0.0 copy-start.2
  5.1 1.6 %copy-done.2 = bf16[64,128,128]{2,1,0:T(8,128)(2,1)S(1)} copy-done((bf16[64,128,128]{2,1,0:T(8,128)(2,1)S(1)}, bf16[64,128,128]{2,1,0:T(8,128)(2,1)}, u32[]{:S(2)}) %copy-start.2) | copy-done | bytes 2097176
  6.7 0.0 copy-start.3
  6.7 0.9 %copy-done.3 = bf16[4,64,256]{2,1,0:T(8,128)(2,1)S(1)} copy-done((bf16[4,64,256]{2,1,0:T(8,128)(2,1)S(1)}, bf16[4,64,256]{2,1,0:T(8,128)(2,1)}, u32[]{:S(2)}) %copy-start.3) | copy-done | bytes 131096
  7.6 0.0 copy-start.6
  7.6 0.8 %copy-done.6 = bf16[4,64,128]{2,1,0:T(8,128)(2,1)S(1)} copy-done((bf16[4,64,128]{2,1,0:T(8,128)(2,1)S(1)}, bf16[4,64,128]{2,1,0:T(8,128)(2,1)}, u32[]{:S(2)}) %copy-start.6) | copy-done | bytes 65560
  8.4 0.0 copy-start.7
  8.4 0.8 %copy-done.7 = bf16[4,64,128]{2,1,0:T(8,128)(2,1)S(1)} copy-done((bf16[4,64,128]{2,1,0:T(8,128)(2,1)S(1)}, bf16[4,64,128]{2,1,0:T(8,128)(2,1)}, u32[]{:S(2)}) %copy-start.7) | copy-done | bytes 65560
  9.3 0.0 copy-start.11
  9.3 0.7 copy-done.11
  9.9 0.0 copy-start
  9.9 0.0 copy-start.4
  9.9 0.0 copy-start.5
  9.9 0.0 copy-start.8
  9.9 0.0 copy-start.9
  9.9 3.2 %shard_map.198.attn = bf16[256,256]{1,0:T(8,128)(2,1)S(1)} custom-call(s32[64]{0:T(128)S(1)} %copy-done.11, bf16[256,256]{1,0:T(8,128)(2,1)S(1)} %bitcast.6, bf16[64,128,128]{2,1,0:T(8,128)(2,1)S(1)} %copy-done.1, bf16[64,128,128]{2,1,0:T(8,128)(2,1)S(1)} %copy-done.2, bf16[256,128]{1,0:T(8,128)(2,1)S(1)} %bitcast.7, bf16[256,128]{1,0:T(8,128)(2,1)S(1)} %bitcast.8), custom_call_target="tpu_custom_call" | custom-call | tf_op jit(solution)/shard_map/pallas_call | solution.py:124
  13.1 0.0 copy-done.10
  13.1 0.0 copy-done
  13.1 0.0 copy-done.4
  13.1 0.0 copy-done.5
  13.2 0.0 copy-done.8
  13.2 0.0 copy-done.9
  13.2 62.2 %shard_map.199 = (bf16[256,256]{1,0:T(8,128)(2,1)S(1)}, f32[256,64]{1,0:T(8,128)S(1)}, f32[64,256]{1,0:T(8,128)S(1)}, f32[256,64]{1,0:T(8,128)S(1)}, f32[256,64]...) custom-call(bf16[256,256]{1,0:T(8,128)(2,1)S(1)} %shard_map.198.attn, bf16[256,256]{1,0:T(8,128)(2,1)S(1)} %copy-done.4, ...), custom_call_target="tpu_custom_call" | custom-call | tf_op jit(solution)/shard_map/pallas_call | solution.py:477
  75.4 0.7 copy.30
  76.1 0.7 copy.26
  76.8 0.7 copy.27
  77.5 0.7 copy.28
  78.2 0.6 copy.34
  78.9 0.6 copy.35
  79.5 0.6 copy.36
  (1 shorter events, 0.0 us)
Async XLA Ops:
  2.5 10.6 %copy-start.10 = (f32[64,256]{1,0:T(8,128)S(1)}, f32[64,256]{1,0:T(8,128)}, u32[]{:S(2)}) copy-start(f32[64,256]{1,0:T(8,128)} %bv_ref.1) | copy-start | bytes 196612
  3.5 1.6 %copy-start.1 = (bf16[64,128,128]{2,1,0:T(8,128)(2,1)S(1)}, bf16[64,128,128]{2,1,0:T(8,128)(2,1)}, u32[]{:S(2)}) copy-start(bf16[64,128,128]{2,1,0:T(8,128)(2,1)} %k_ref.1) | copy-start | bytes 6291460
  5.1 1.6 %copy-start.2 = (bf16[64,128,128]{2,1,0:T(8,128)(2,1)S(1)}, bf16[64,128,128]{2,1,0:T(8,128)(2,1)}, u32[]{:S(2)}) copy-start(bf16[64,128,128]{2,1,0:T(8,128)(2,1)} %v_ref.1) | copy-start | bytes 6291460
  6.7 0.9 %copy-start.3 = (bf16[4,64,256]{2,1,0:T(8,128)(2,1)S(1)}, bf16[4,64,256]{2,1,0:T(8,128)(2,1)}, u32[]{:S(2)}) copy-start(bf16[4,64,256]{2,1,0:T(8,128)(2,1)} %param.24) | copy-start | bytes 393220
  7.6 0.8 %copy-start.6 = (bf16[4,64,128]{2,1,0:T(8,128)(2,1)S(1)}, bf16[4,64,128]{2,1,0:T(8,128)(2,1)}, u32[]{:S(2)}) copy-start(bf16[4,64,128]{2,1,0:T(8,128)(2,1)} %param.27) | copy-start | bytes 196612
  8.4 0.8 %copy-start.7 = (bf16[4,64,128]{2,1,0:T(8,128)(2,1)S(1)}, bf16[4,64,128]{2,1,0:T(8,128)(2,1)}, u32[]{:S(2)}) copy-start(bf16[4,64,128]{2,1,0:T(8,128)(2,1)} %param.28) | copy-start | bytes 196612
  9.3 0.7 copy-start.11
  9.9 3.2 %copy-start = (bf16[256,8192]{1,0:T(8,128)(2,1)S(1)}, bf16[256,8192]{1,0:T(8,128)(2,1)}, u32[]{:S(2)}) copy-start(bf16[256,8192]{1,0:T(8,128)(2,1)} %w_hbm.1) | copy-start | bytes 12582916
  9.9 3.2 %copy-start.4 = (bf16[256,256]{1,0:T(8,128)(2,1)S(1)}, bf16[256,256]{1,0:T(8,128)(2,1)}, u32[]{:S(2)}) copy-start(bf16[256,256]{1,0:T(8,128)(2,1)} %x.1) | copy-start | bytes 393220
  9.9 3.2 %copy-start.5 = (bf16[256,256]{1,0:T(8,128)(2,1)S(1)}, bf16[256,256]{1,0:T(8,128)(2,1)}, u32[]{:S(2)}) copy-start(bf16[256,256]{1,0:T(8,128)(2,1)} %dy.1) | copy-start | bytes 393220
  9.9 3.2 %copy-start.8 = (f32[64,256]{1,0:T(8,128)S(1)}, f32[64,256]{1,0:T(8,128)}, u32[]{:S(2)}) copy-start(f32[64,256]{1,0:T(8,128)} %b_ref.1) | copy-start | bytes 196612
  9.9 3.2 %copy-start.9 = (f32[64,256]{1,0:T(8,128)S(1)}, f32[64,256]{1,0:T(8,128)}, u32[]{:S(2)}) copy-start(f32[64,256]{1,0:T(8,128)} %bm_ref.1) | copy-start | bytes 196612

commit v2 on v1

--- a/solution.py
+++ b/solution.py
@@ -54,97 +54,87 @@
     return high, low
 
 
-def attention_kernel(
-    len_ref, q_ref, k_ref, v_ref, fk_ref, fv_ref, out_ref, qs, sc, sn, wc, mixed
-):
-    pairs = k_ref.shape[0] // 2
-    inv_root = 1.0 / math.sqrt(128)
-    i0 = lax.broadcasted_iota(jnp.int32, (ROWS, ROWS), 0)
-    i1 = lax.broadcasted_iota(jnp.int32, (ROWS, ROWS), 1)
-    perm = jnp.where(i1 == (i0 % 4) * 64 + i0 // 4, 1.0, 0.0).astype(BF16)
-    qp = dot(perm, q_ref[...])
-    qp = jnp.concatenate(
-        [qp[:, :128].reshape(pairs, 8, 128), qp[:, 128:].reshape(pairs, 8, 128)], axis=1
-    )
-    qs[...] = qp.reshape(pairs * 16, 128).astype(BF16)
-    fk = dot(perm, fk_ref[...]).astype(BF16)
-    fv = dot(perm, fv_ref[...]).astype(BF16)
-
-    row = lax.broadcasted_iota(jnp.int32, (16, 256), 0)
-    col = lax.broadcasted_iota(jnp.int32, (16, 256), 1)
-    second = (row // 4) % 2 == 1
-
-    def scores(p, carry):
-        keys = k_ref[pl.ds(2 * p, 2)].reshape(256, 128)
-        at = pl.ds(pl.multiple_of(p * 16, 16), 16)
-        s = dot_t(qs[at, :], keys) * inv_root
+class Attention:
+    def __init__(self, lengths, q, k, v, fk, fv, out, qs, sc, sn, wc, mixed):
+        self.lengths, self.q, self.k, self.v, self.fk, self.fv = lengths, q, k, v, fk, fv
+        self.out, self.qs, self.sc, self.sn, self.wc, self.mixed = out, qs, sc, sn, wc, mixed
+        self.pairs = k.shape[0] // 2
+        i0 = lax.broadcasted_iota(jnp.int32, (ROWS, ROWS), 0)
+        i1 = lax.broadcasted_iota(jnp.int32, (ROWS, ROWS), 1)
+        self.perm = jnp.where(i1 == (i0 % 4) * 64 + i0 // 4, 1.0, 0.0).astype(BF16)
+
+    def scores(self):
+        pairs, qs, sc, sn = self.pairs, self.qs, self.sc, self.sn
+        inv_root = 1.0 / math.sqrt(128)
+        qp = dot(self.perm, self.q[...])
+        qp = jnp.concatenate(
+            [qp[:, :128].reshape(pairs, 8, 128), qp[:, 128:].reshape(pairs, 8, 128)], axis=1
+        )
+        qs[...] = qp.reshape(pairs * 16, 128).astype(BF16)
+        fk = dot(self.perm, self.fk[...]).astype(BF16)
+
+        row = lax.broadcasted_iota(jnp.int32, (16, 256), 0)
+        col = lax.broadcasted_iota(jnp.int32, (16, 256), 1)
+        second = (row // 4) % 2 == 1
         start = jnp.where(second, 128, 0)
-        stop = jnp.where(second, 128 + len_ref[2 * p + 1], len_ref[2 * p])
-        sc[at, :] = jnp.where((col >= start) & (col < stop), s, -jnp.inf)
-        return carry
-
-    lax.fori_loop(0, pairs, scores, 0, unroll=8)
-
-    nrow = lax.broadcasted_iota(jnp.int32, (256, 128), 0)
-    ncol = lax.broadcasted_iota(jnp.int32, (256, 128), 1)
-    request = (nrow // 16) * 2 + (nrow // 4) % 2
-    new_live = (ncol // 4 == request) & (ncol % 4 <= nrow % 4)
-    for half in range(2):
-        part = pl.ds(half * 256, 256)
-        s = dot_t(qs[part, :], fk[half * 128 : half * 128 + 128]) * inv_root
-        sn[part, :] = jnp.where(new_live, s, -jnp.inf)
-
-    for block in range(8):
-        part = pl.ds(block * 64, 64)
-        s, n = sc[part, :], sn[part, :]
-        largest = jnp.maximum(
-            jnp.max(s, axis=1, keepdims=True), jnp.max(n, axis=1, keepdims=True)
-        )
-        e, m = jnp.exp(s - largest), jnp.exp(n - largest)
-        total = jnp.sum(e, axis=1, keepdims=True) + jnp.sum(m, axis=1, keepdims=True)
-        scale = 1.0 / total
-        wc[part, :] = (e * scale).astype(BF16)
-        where_new = (block // 4) * 128
-        mixed[part, :] = dot((m * scale).astype(BF16), fv[where_new : where_new + 128])
-
-    def mix(p, carry):
-        values = v_ref[pl.ds(2 * p, 2)].reshape(256, 128)
-        at = pl.ds(pl.multiple_of(p * 16, 16), 16)
-        mixed[at, :] += dot(wc[at, :], values)
-        return carry
-
-    lax.fori_loop(0, pairs, mix, 0, unroll=8)
-    o = mixed[...].reshape(pairs, 16, 128)
-    out_ref[:, :128] = o[:, :8].reshape(ROWS, 128).astype(BF16)
-    out_ref[:, 128:] = o[:, 8:].reshape(ROWS, 128).astype(BF16)
-
-
-def attention(lengths, queries, keys, values, fresh_keys, fresh_values):
-    vmem = pl.BlockSpec(memory_space=pltpu.VMEM)
-    return pl.pallas_call(
-        attention_kernel,
-        out_shape=jax.ShapeDtypeStruct((ROWS, FEAT), BF16),
-        in_specs=[pl.BlockSpec(memory_space=pltpu.SMEM)] + [vmem] * 5,
-        out_specs=vmem,
-        scratch_shapes=[
-            pltpu.VMEM((512, 128), BF16),
-            pltpu.VMEM((512, 256), F32),
-            pltpu.VMEM((512, 128), F32),
-            pltpu.VMEM((512, 256), BF16),
-            pltpu.VMEM((512, 128), F32),
-        ],
-        compiler_params=pltpu.CompilerParams(vmem_limit_bytes=24 * 1024 * 1024),
-    )(lengths, queries, keys, values, fresh_keys, fresh_values)
+
+        def one_pair(p, carry):
+            keys = self.k[pl.ds(2 * p, 2)].reshape(256, 128)
+            at = pl.ds(pl.multiple_of(p * 16, 16), 16)
+            s = dot_t(qs[at, :], keys) * inv_root
+            stop = jnp.where(second, 128 + self.lengths[2 * p + 1], self.lengths[2 * p])
+            sc[at, :] = jnp.where((col >= start) & (col < stop), s, -jnp.inf)
+            return carry
+
+        lax.fori_loop(0, pairs, one_pair, 0, unroll=8)
+
+        nrow = lax.broadcasted_iota(jnp.int32, (256, 128), 0)
+        ncol = lax.broadcasted_iota(jnp.int32, (256, 128), 1)
+        request = (nrow // 16) * 2 + (nrow // 4) % 2
+        new_live = (ncol // 4 == request) & (ncol % 4 <= nrow % 4)
+        for half in range(2):
+            part = pl.ds(half * 256, 256)
+            s = dot_t(qs[part, :], fk[half * 128 : half * 128 + 128]) * inv_root
+            sn[part, :] = jnp.where(new_live, s, -jnp.inf)
+
+    def mix(self):
+        pairs, sc, sn, wc, mixed = self.pairs, self.sc, self.sn, self.wc, self.mixed
+        fv = dot(self.perm, self.fv[...]).astype(BF16)
+        for block in range(8):
+            part = pl.ds(block * 64, 64)
+            s, n = sc[part, :], sn[part, :]
+            largest = jnp.maximum(
+                jnp.max(s, axis=1, keepdims=True), jnp.max(n, axis=1, keepdims=True)
+            )
+            e, m = jnp.exp(s - largest), jnp.exp(n - largest)
+            total = jnp.sum(e, axis=1, keepdims=True) + jnp.sum(m, axis=1, keepdims=True)
+            scale = 1.0 / total
+            wc[part, :] = (e * scale).astype(BF16)
+            where_new = (block // 4) * 128
+            mixed[part, :] = dot((m * scale).astype(BF16), fv[where_new : where_new + 128])
+
+        def one_pair(p, carry):
+            values = self.v[pl.ds(2 * p, 2)].reshape(256, 128)
+            at = pl.ds(pl.multiple_of(p * 16, 16), 16)
+            mixed[at, :] += dot(wc[at, :], values)
+            return carry
+
+        lax.fori_loop(0, pairs, one_pair, 0, unroll=8)
+        o = mixed[...].reshape(pairs, 16, 128)
+        self.out[:, :128] = o[:, :8].reshape(ROWS, 128).astype(BF16)
+        self.out[:, 128:] = o[:, 8:].reshape(ROWS, 128).astype(BF16)
 
 
 def step_kernel(
-    attn, x, dy, a_ref, b_ref, am_ref, av_ref, bm_ref, bv_ref, w_hbm,
+    x_h, dy_h, a_h, b_h, len_h, q_h, fk_h, k_h, fv_h, v_h, w_h, am_h, av_h, bm_h, bv_h,
     dec, a_out, b_out, am_out, av_out, bm_out, bv_out,
-    w, csend, crecv, ysend, yrecv, zsa, zra, zsb, zrb, yfin,
+    x, dy, a_ref, b_ref, lengths, q, fk, keys, fv, values, w, am_ref, av_ref, bm_ref, bv_ref,
+    attn, summed, qs, sc, sn, wc, mixed,
+    csend, crecv, ysend, yrecv, zsa, zra, zsb, zrb, yfin,
     one_in, one_z, one_g, one_gr, one_out,
     grad, grad_r, grad_out,
     two_in, two_z, two_g, two_gr, two_out,
-    w_sem, c_s, c_r, y_s, y_r, za_s, za_r, zb_s, zb_r, yf_s, yf_r, t_s, t_r,
+    in_sem, c_s, c_r, y_s, y_r, za_s, za_r, zb_s, zb_r, yf_s, yf_r, t_s, t_r,
 ):
     d = lax.axis_index("dp")
     t = lax.axis_index("tensor")
@@ -159,8 +149,14 @@
     group = [core_peer, y_peer, at(z, 1 - y, 1 - c)]
     dp_peers = [(lax.rem(d + k, DP), t) for k in range(1, DP)]
 
-    load_w = pltpu.make_async_copy(w_hbm, w, w_sem)
-    load_w.start()
+    here = (x, dy, a_ref, b_ref, lengths, q, fk, keys, fv, values, w, am_ref, av_ref, bm_ref, bv_ref)
+    there = (x_h, dy_h, a_h, b_h, len_h, q_h, fk_h, k_h, fv_h, v_h, w_h, am_h, av_h, bm_h, bv_h)
+    loads = [
+        pltpu.make_async_copy(src, dst, in_sem.at[i])
+        for i, (src, dst) in enumerate(zip(there, here))
+    ]
+    for load in loads:
+        load.start()
 
     barrier = pltpu.get_barrier_semaphore()
     everyone = z_peers + group + dp_peers
@@ -237,11 +233,13 @@
     sum_one = TensorSum(one_in, one_z, one_g, one_gr, one_out, 0)
     sum_two = TensorSum(two_in, two_z, two_g, two_gr, two_out, 17)
 
+    for load in loads[:4]:
+        load.wait()
     a_high, a_low = two_terms(a_ref[...])
     b_high, b_low = two_terms(b_ref[...])
     one_in[...] = jnp.concatenate(
         [
-            dot(x[...], a_high) + dot(x[...], a_low),
+            dot_t(x[...], a_high) + dot_t(x[...], a_low),
             dot_t(dy[...], b_high) + dot_t(dy[...], b_low),
         ],
         axis=1,
@@ -287,7 +285,7 @@
         for k in range(1, DP):
             grad_gather(k).wait_recv()
         new_a, a_one, a_two = apply_adam_step(
-            a_ref[...], am_ref[...], av_ref[...], grad_out[:RANK, :].T
+            a_ref[...], am_ref[...], av_ref[...], grad_out[:RANK, :]
         )
         a_out[...], am_out[...], av_out[...] = new_a, a_one, a_two
         new_b, b_one, b_two = apply_adam_step(
@@ -295,7 +293,7 @@
         )
         b_out[...], bm_out[...], bv_out[...] = new_b, b_one, b_two
         high, low = two_terms(new_a)
-        two_in[...] = dot(attn[...], jnp.concatenate([high, low], axis=1))
+        two_in[...] = dot_t(attn[...], jnp.concatenate([high, low], axis=0))
         sum_two.one()
 
     up, down = lax.rem(z + 1, ZN), lax.rem(z + ZN - 1, ZN)
@@ -386,19 +384,28 @@
             def _():
                 zb_copy(step, side).start()
 
-    load_w.wait()
+    attend = Attention(lengths, q, keys, values, fk, fv, attn, qs, sc, sn, wc, mixed)
+    for load in loads[4:8]:
+        load.wait()
+    attend.scores()
+    sum_one.two()
+    for load in loads[8:10]:
+        load.wait()
+    attend.mix()
+    sum_one.three()
+    loads[10].wait()
     core_stage(0)
     core_stage(1)
     y_stage(0)
-    sum_one.two()
+    for load in loads[11:]:
+        load.wait()
 
     at_step = {
-        0: sum_one.three,
-        1: gradients,
-        2: gradient_sum,
-        3: update,
-        4: sum_two.two,
-        5: sum_two.three,
+        0: gradients,
+        1: gradient_sum,
+        2: update,
+        3: sum_two.two,
+        4: sum_two.three,
     }
 
     def ring(step, carry):
@@ -429,15 +436,20 @@
 
     for side in range(2):
         rows_b = pl.ds(side * HALF + ROWS_A, ROWS_B)
-        dec[rows_b, :] = (
+        summed[rows_b, :] = (
             zsb[ZN - 1, side] + delta[side * HALF + ROWS_A : (side + 1) * HALF]
         ).astype(BF16)
     for side in range(2):
         yfin_copy(side).wait_recv()
         rows_a = pl.ds(side * HALF, ROWS_A)
-        dec[rows_a, :] = (
+        summed[rows_a, :] = (
             (zsa[ZN - 1, side, 0] + yfin[side]) + delta[side * HALF : side * HALF + ROWS_A]
         ).astype(BF16)
+
+    back = lax.dot_general(
+        attend.perm, summed[...], (((0,), (0,)), ((), ())), preferred_element_type=F32
+    )
+    dec[...] = back.astype(BF16)
 
     sum_one.finish()
     sum_two.finish()
@@ -462,11 +474,11 @@
     lax.fori_loop(0, ZN, drain, 0)
 
 
-def step(attn, x, dy, a, b, am, av, bm, bv, weight):
+def step(*args):
     vmem = pl.BlockSpec(memory_space=pltpu.VMEM)
-    down = jax.ShapeDtypeStruct((FEAT, RANK), F32)
-    up = jax.ShapeDtypeStruct((RANK, FEAT), F32)
+    factor = jax.ShapeDtypeStruct((RANK, FEAT), F32)
     dma = pltpu.SemaphoreType.DMA
+    places = [pltpu.SMEM if arg.ndim == 1 else pltpu.VMEM for arg in args]
     small = [
         pltpu.VMEM((256, 128), F32),
         pltpu.VMEM((7, 32, 128), F32),
@@ -476,13 +488,18 @@
     ]
     return pl.pallas_call(
         step_kernel,
-        out_shape=(
-            jax.ShapeDtypeStruct((ROWS, FEAT), BF16), down, up, down, down, up, up
-        ),
-        in_specs=[vmem] * 9 + [pl.BlockSpec(memory_space=pl.ANY)],
+        out_shape=(jax.ShapeDtypeStruct((ROWS, FEAT), BF16),) + (factor,) * 6,
+        in_specs=[pl.BlockSpec(memory_space=pltpu.HBM)] * len(args),
         out_specs=(vmem,) * 7,
         scratch_shapes=[
-            pltpu.VMEM((FEAT, 8192), BF16),
+            *[place(arg.shape, arg.dtype) for place, arg in zip(places, args)],
+            pltpu.VMEM((ROWS, FEAT), BF16),
+            pltpu.VMEM((ROWS, FEAT), BF16),
+            pltpu.VMEM((512, 128), BF16),
+            pltpu.VMEM((512, 256), F32),
+            pltpu.VMEM((512, 128), F32),
+            pltpu.VMEM((512, 256), BF16),
+            pltpu.VMEM((512, 128), F32),
             pltpu.VMEM((ZN, 2, 2, HALF, FEAT), F32),
             pltpu.VMEM((ZN, 2, 2, HALF, FEAT), F32),
             pltpu.VMEM((ZN, 2, ROWS_B, FEAT), F32),
@@ -497,16 +514,39 @@
             pltpu.VMEM((7, 16, FEAT), F32),
             pltpu.VMEM((128, FEAT), F32),
             *small,
-            dma,
+            dma((len(args),)),
             dma((ZN, 2)), dma((ZN, 2)), dma((ZN, 2)), dma((ZN, 2)),
             dma((ZN - 1, 2)), dma((ZN - 1, 2)), dma((ZN - 1, 2)), dma((ZN - 1, 2)),
             dma((2,)), dma((2,)),
             dma((48,)), dma((48,)),
         ],
         compiler_params=pltpu.CompilerParams(
-            collective_id=0, has_side_effects=True, vmem_limit_bytes=40 * 1024 * 1024
+            collective_id=0, has_side_effects=True, vmem_limit_bytes=64 * 1024 * 1024
         ),
-    )(attn, x, dy, a, b, am, av, bm, bv, weight)
+    )(*args)
+
+
+def hand_out_kernel(*refs):
+    half = len(refs) // 2
+    copies = [
+        pltpu.make_async_copy(src, dst, refs[-1].at[i])
+        for i, (src, dst) in enumerate(zip(refs[:half], refs[half:-1]))
+    ]
+    for copy in copies:
+        copy.start()
+    for copy in copies:
+        copy.wait()
+
+
+def hand_out(*args):
+    return pl.pallas_call(
+        hand_out_kernel,
+        out_shape=tuple(jax.ShapeDtypeStruct(arg.shape, arg.dtype) for arg in args),
+        in_specs=[pl.BlockSpec(memory_space=pl.ANY)] * len(args),
+        out_specs=(pl.BlockSpec(memory_space=pltpu.HBM),) * len(args),
+        scratch_shapes=[pltpu.SemaphoreType.DMA((len(args),))],
+        compiler_params=pltpu.CompilerParams(vmem_limit_bytes=64 * 1024 * 1024),
+    )(*args)
 
 
 def per_device(
@@ -526,29 +566,27 @@
     fresh_values,
     lengths,
 ):
-    attn = attention(
+    results = step(
+        projection_input,
+        output_gradient,
+        adapter_down.T,
+        adapter_up,
         lengths,
         queries.reshape(ROWS, FEAT),
+        fresh_keys.reshape(ROWS, 128),
         stored_keys,
+        fresh_values.reshape(ROWS, 128),
         stored_values,
-        fresh_keys.reshape(ROWS, 128),
-        fresh_values.reshape(ROWS, 128),
-    )
-    decoded, *rest = step(
-        attn,
-        projection_input,
-        output_gradient,
-        adapter_down,
-        adapter_up,
-        down_first_moment,
-        down_second_moment,
+        projection_weight,
+        down_first_moment.T,
+        down_second_moment.T,
         up_first_moment,
         up_second_moment,
-        projection_weight,
     )
-    decoded = decoded.reshape(64, 4, FEAT).transpose(1, 0, 2)
-    new_a, new_b, a_one, a_two, b_one, b_two = rest
-    return (decoded, new_a, new_b, a_one, a_two, b_one, b_two)
+    decoded, new_a, new_b, a_one, a_two, b_one, b_two = hand_out(*results)
+    return (
+        decoded.reshape(queries.shape), new_a.T, new_b, a_one.T, a_two.T, b_one, b_two
+    )
 
 
 def solution(mesh):

time: 80.5 us -> 88.4 us (1.098)
  the two profiles are of different devices: /device:TPU:72 before, /device:TPU:32 now
where the time goes in v2:
time: 88.4 us; the launch traced here: 88.3 us
  Pallas kernels  87.7 us (99%)
    pallas_call x1, Pallas kernels, step(): pl.pallas_call(step_kernel, out_shape=(jax.ShapeDtypeStruct((ROWS, FEAT),...  70.6 us
    pallas_call x1, Pallas kernels, hand_out(): pl.pallas_call(hand_out_kernel, out_shape=tuple((jax.ShapeDtypeStruct(arg...  17.1 us

profile of v2, /device:TPU:32, one launch (start us, length us, event | category | flops | bytes accessed | tf_op | source)
XLA Modules:
  0.0 88.3 jit_solution(16178990786191776579)
XLA Ops:
  0.6 70.6 %shard_map.198 = (bf16[256,256]{1,0:T(8,128)(2,1)}, f32[64,256]{1,0:T(8,128)}, f32[64,256]{1,0:T(8,128)}, f32[64,256]{1,0:T(8,128)}, f32[64,256]{1,0:T(8,128)}, /*index=5*/f32[64,256]{1,0:T(8,128)}, f32[64,256]{1,0:T(8,128)}) custom-call(bf16[256,256]{1,0:T(8,128)(2,1)} %x_h.1, bf16[256,256]{1,0:T(8,128)(2,1)} %dy_h.1, f32[64,256]{1,0:T(8,128)} %bitcast.11, ...), custom_call_target="tpu_custom_call" | custom-call | tf_op jit(solution)/shard_map/pallas_call | solution.py:489
  71.3 17.1 %shard_map.199 = (bf16[256,256]{1,0:T(8,128)(2,1)}, f32[64,256]{1,0:T(8,128)}, f32[64,256]{1,0:T(8,128)}, f32[64,256]{1,0:T(8,128)}, f32[64,256]{1,0:T(8,128)}, /*index=5*/f32[64,256]{1,0:T(8,128)}, f32[64,256]{1,0:T(8,128)}) custom-call(bf16[256,256]{1,0:T(8,128)(2,1)} %get-tuple-element.21.refs_0_, f32[64,256]{1,0:T(8,128)} %get-tuple-element.22.refs_1_, ...), custom_call_target="tpu_custom_call" | custom-call | tf_op jit(solution)/shard_map/pallas_call | solution.py:542

commit v3 on v2

--- a/solution.py
+++ b/solution.py
@@ -23,10 +23,11 @@
 FEAT = 256
 RANK = 64
 ZN = 8
+CHIPS = 16
 DP = 8
 HALF = ROWS // 2
-ROWS_A = 64
-ROWS_B = HALF - ROWS_A
+FIRST = 64
+STREAMS = (pl.ds(0, FIRST), pl.ds(FIRST, FIRST), pl.ds(2 * FIRST, HALF - FIRST))
 
 
 def apply_adam_step(current, moment_one, moment_two, gradient):
@@ -130,11 +131,11 @@
     dec, a_out, b_out, am_out, av_out, bm_out, bv_out,
     x, dy, a_ref, b_ref, lengths, q, fk, keys, fv, values, w, am_ref, av_ref, bm_ref, bv_ref,
     attn, summed, qs, sc, sn, wc, mixed,
-    csend, crecv, ysend, yrecv, zsa, zra, zsb, zrb, yfin,
-    one_in, one_z, one_g, one_gr, one_out,
+    csend, crecv, ysend, yrecv, zs, zr, yfin_src, yfin,
+    one_in, one_core, one_half, one_recv, one_out,
     grad, grad_r, grad_out,
-    two_in, two_z, two_g, two_gr, two_out,
-    in_sem, c_s, c_r, y_s, y_r, za_s, za_r, zb_s, zb_r, yf_s, yf_r, t_s, t_r,
+    two_in, two_core, two_half, two_recv, two_out,
+    in_sem, c_s, c_r, y_s, y_r, z_s, z_r, yf_s, yf_r, t_s, t_r,
 ):
     d = lax.axis_index("dp")
     t = lax.axis_index("tensor")
@@ -145,8 +146,8 @@
 
     core_peer = at(z, y, 1 - c)
     y_peer = at(z, 1 - y, c)
-    z_peers = [at(lax.rem(z + k, ZN), y, c) for k in range(1, ZN)]
-    group = [core_peer, y_peer, at(z, 1 - y, 1 - c)]
+    chip = z * 2 + y
+    chip_peers = [(d, lax.rem(chip + k, CHIPS) * 2 + c) for k in range(1, CHIPS)]
     dp_peers = [(lax.rem(d + k, DP), t) for k in range(1, DP)]
 
     here = (x, dy, a_ref, b_ref, lengths, q, fk, keys, fv, values, w, am_ref, av_ref, bm_ref, bv_ref)
@@ -159,7 +160,7 @@
         load.start()
 
     barrier = pltpu.get_barrier_semaphore()
-    everyone = z_peers + group + dp_peers
+    everyone = chip_peers + [core_peer] + dp_peers
     for peer in everyone:
         pl.semaphore_signal(barrier, inc=1, device_id=peer, device_id_type=MESH)
 
@@ -174,64 +175,74 @@
         )
 
     class TensorSum:
-        def __init__(self, src, z_recv, mine, g_recv, out, first):
-            self.src, self.z_recv, self.mine = src, z_recv, mine
-            self.g_recv, self.out, self.first = g_recv, out, first
-            self.here = pl.ds(pl.multiple_of(z * 32, 32), 32)
+        def __init__(self, src, core_recv, half, recv, out, first):
+            self.src, self.core_recv, self.half = src, core_recv, half
+            self.recv, self.out, self.first = recv, out, first
+            self.mine = pl.ds(pl.multiple_of(c * 128, 128), 128)
+            self.theirs = pl.ds(pl.multiple_of((1 - c) * 128, 128), 128)
+            self.part = pl.ds(pl.multiple_of(chip * 8, 8), 8)
+            self.here = pl.ds(pl.multiple_of(c * 128 + chip * 8, 8), 8)
+
+        def core_scatter(self):
+            i = self.first
+            return remote(self.src.at[self.theirs], self.core_recv, t_s.at[i], t_r.at[i], core_peer)
 
         def scatter(self, k):
-            part = pl.ds(pl.multiple_of(lax.rem(z + k, ZN) * 32, 32), 32)
-            i = self.first + k - 1
+            part = pl.ds(pl.multiple_of(lax.rem(chip + k, CHIPS) * 8, 8), 8)
+            i = self.first + k
             return remote(
-                self.src.at[part], self.z_recv.at[k - 1], t_s.at[i], t_r.at[i], z_peers[k - 1]
+                self.half.at[part], self.recv.at[k - 1], t_s.at[i], t_r.at[i], chip_peers[k - 1]
             )
 
-        def exchange(self, m):
-            i = self.first + 7 + m
-            return remote(self.mine, self.g_recv.at[m], t_s.at[i], t_r.at[i], group[m])
-
         def gather(self, k):
-            i = self.first + 10 + k - 1
+            i = self.first + 15 + k
             return remote(
-                self.out.at[self.here], self.out.at[self.here], t_s.at[i], t_r.at[i], z_peers[k - 1]
+                self.out.at[self.here], self.out.at[self.here],
+                t_s.at[i], t_r.at[i], chip_peers[k - 1],
             )
 
+        def core_gather(self):
+            i = self.first + 31
+            return remote(
+                self.out.at[self.mine], self.out.at[self.mine], t_s.at[i], t_r.at[i], core_peer
+            )
+
         def one(self):
-            for k in range(1, ZN):
+            self.core_scatter().start()
+
+        def two(self):
+            self.core_scatter().wait_recv()
+            self.half[...] = self.src[self.mine, :] + self.core_recv[...]
+            for k in range(1, CHIPS):
                 self.scatter(k).start()
 
-        def two(self):
-            for k in range(1, ZN):
+        def three(self):
+            for k in range(1, CHIPS):
                 self.scatter(k).wait_recv()
-            total = self.src[self.here, :]
-            for k in range(1, ZN):
-                total = total + self.z_recv[k - 1]
-            self.mine[...] = total
-            for m in range(3):
-                self.exchange(m).start()
-
-        def three(self):
-            for m in range(3):
-                self.exchange(m).wait_recv()
-            self.out[self.here, :] = (self.mine[...] + self.g_recv[0]) + (
-                self.g_recv[1] + self.g_recv[2]
-            )
-            for k in range(1, ZN):
+            total = self.half[self.part, :]
+            for k in range(1, CHIPS):
+                total = total + self.recv[k - 1]
+            self.out[self.here, :] = total
+            for k in range(1, CHIPS):
                 self.gather(k).start()
 
         def four(self):
-            for k in range(1, ZN):
+            for k in range(1, CHIPS):
                 self.gather(k).wait_recv()
+            self.core_gather().start()
+
+        def five(self):
+            self.core_gather().wait_recv()
 
         def finish(self):
-            for k in range(1, ZN):
+            self.core_scatter().wait_send()
+            self.core_gather().wait_send()
+            for k in range(1, CHIPS):
                 self.scatter(k).wait_send()
                 self.gather(k).wait_send()
-            for m in range(3):
-                self.exchange(m).wait_send()
-
-    sum_one = TensorSum(one_in, one_z, one_g, one_gr, one_out, 0)
-    sum_two = TensorSum(two_in, two_z, two_g, two_gr, two_out, 17)
+
+    sum_one = TensorSum(one_in, one_core, one_half, one_recv, one_out, 0)
+    sum_two = TensorSum(two_in, two_core, two_half, two_recv, two_out, 32)
 
     for load in loads[:4]:
         load.wait()
@@ -251,17 +262,17 @@
 
     def grad_scatter(k):
         part = pl.ds(pl.multiple_of(lax.rem(d + k, DP) * 16, 16), 16)
-        i = 34 + k - 1
+        i = 64 + k - 1
         return remote(grad.at[part], grad_r.at[k - 1], t_s.at[i], t_r.at[i], dp_peers[k - 1])
 
     def grad_gather(k):
-        i = 41 + k - 1
+        i = 71 + k - 1
         return remote(
             grad_out.at[d_here], grad_out.at[d_here], t_s.at[i], t_r.at[i], dp_peers[k - 1]
         )
 
     def gradients():
-        sum_one.four()
+        sum_one.five()
         scale = adapter_scale / (ROWS * DP)
         both = one_out[...].T
         x_high, x_low = two_terms(both[:RANK])
@@ -288,164 +299,169 @@
             a_ref[...], am_ref[...], av_ref[...], grad_out[:RANK, :]
         )
         a_out[...], am_out[...], av_out[...] = new_a, a_one, a_two
+        high, low = two_terms(new_a)
+        two_in[...] = dot_t(attn[...], jnp.concatenate([high, low], axis=0))
+        sum_two.one()
         new_b, b_one, b_two = apply_adam_step(
             b_ref[...], bm_ref[...], bv_ref[...], grad_out[RANK:, :]
         )
         b_out[...], bm_out[...], bv_out[...] = new_b, b_one, b_two
-        high, low = two_terms(new_a)
-        two_in[...] = dot_t(attn[...], jnp.concatenate([high, low], axis=0))
-        sum_two.one()
-
-    up, down = lax.rem(z + 1, ZN), lax.rem(z + ZN - 1, ZN)
-    sides = [at(up, y, c), at(down, y, c)]
-
-    def destination(step, side):
-        return lax.rem(z + 2 * ZN - 1 - step, ZN) if side == 0 else lax.rem(z + 1 + step, ZN)
-
-    def product(step, side, other_y, other_c):
+
+    ways = [at(lax.rem(z + 1, ZN), y, c), at(lax.rem(z + ZN - 1, ZN), y, c)]
+
+    def product(u, other_y, other_c):
         yy = (1 - y) if other_y else y
         cc = (1 - c) if other_c else c
-        block = (destination(step, side) * 2 + yy) * 2 + cc
+        to = lax.rem(z + ZN + 4 + (1 - 2 * lax.rem(u, 2)) * ((u + 1) // 2), ZN)
+        block = (to * 2 + yy) * 2 + cc
         cols = pl.ds(pl.multiple_of(block * FEAT, FEAT), FEAT)
-        return dot(attn[pl.ds(side * HALF, HALF), :], w[:, cols])
-
-    def core_copy(step, side):
+        return dot(attn[...], w[:, cols])
+
+    def core_copy(u):
+        return remote(csend.at[u], crecv.at[u], c_s.at[u], c_r.at[u], core_peer)
+
+    def y_copy(u):
+        return remote(ysend.at[u], yrecv.at[u], y_s.at[u], y_r.at[u], y_peer)
+
+    def core_stage(u):
+        for k in range(2):
+            csend[u, k] = product(u, k == 1, True)
+        core_copy(u).start()
+
+    def y_stage(u):
+        own = product(u, False, False)
+        other = product(u, True, False)
+        core_copy(u).wait_recv()
+        own = own + crecv[u, 0]
+        other = other + crecv[u, 1]
+        for half in range(2):
+            low, mid, high = half * HALF, half * HALF + FIRST, (half + 1) * HALF
+            ysend[u, half] = other[mid:high]
+            zs[u, half, STREAMS[0], :] = other[low:mid]
+            zs[u, half, STREAMS[1], :] = own[low:mid]
+            zs[u, half, STREAMS[2], :] = own[mid:high]
+        y_copy(u).start()
+
+    def y_add(u):
+        y_copy(u).wait_recv()
+        for half in range(2):
+            zs[u, half, STREAMS[2], :] += yrecv[u, half]
+
+    def unit(step, way):
+        return 0 if step == 0 else 2 * step - 1 + way
+
+    def z_copy(step, way, half, stream):
         return remote(
-            csend.at[step, side], crecv.at[step, side],
-            c_s.at[step, side], c_r.at[step, side], core_peer,
+            zs.at[unit(step, way), half, STREAMS[stream]],
+            zr.at[step, way, half, STREAMS[stream]],
+            z_s.at[step, way, half, stream],
+            z_r.at[step, way, half, stream],
+            ways[way],
         )
 
-    def y_copy(step, side):
-        return remote(
-            ysend.at[step, side], yrecv.at[step, side],
-            y_s.at[step, side], y_r.at[step, side], y_peer,
-        )
-
-    def za_copy(step, side):
-        return remote(
-            zsa.at[step, side], zra.at[step, side],
-            za_s.at[step, side], za_r.at[step, side], sides[side],
-        )
-
-    def zb_copy(step, side):
-        return remote(
-            zsb.at[step, side], zrb.at[step, side],
-            zb_s.at[step, side], zb_r.at[step, side], sides[side],
-        )
-
-    def yfin_copy(side):
-        return remote(
-            zsa.at[ZN - 1, side, 1], yfin.at[side], yf_s.at[side], yf_r.at[side], y_peer
-        )
-
-    def core_stage(step):
-        for side in range(2):
-            for k in range(2):
-                csend[step, side, k] = product(step, side, k == 1, True)
-            core_copy(step, side).start()
-
-    def y_stage(step):
-        for side in range(2):
-            own = product(step, side, False, False)
-            other = product(step, side, True, False)
-            core_copy(step, side).wait_recv()
-            own = own + crecv[step, side, 0]
-            other = other + crecv[step, side, 1]
-            ysend[step, side] = other[ROWS_A:]
-            y_copy(step, side).start()
-            zsa[step, side, 0] = own[:ROWS_A]
-            zsa[step, side, 1] = other[:ROWS_A]
-            zsb[step, side] = own[ROWS_A:]
-
-    def z_stage(step):
-        for side in range(2):
-            @pl.when(step > 0)
-            def _():
-                za_copy(step - 1, side).wait_recv()
-                zsa[step, side] += zra[step - 1, side]
-
-            @pl.when(step < ZN - 1)
-            def _():
-                za_copy(step, side).start()
-
-        for side in range(2):
-            y_copy(step, side).wait_recv()
-
-            @pl.when(step > 0)
-            def _():
-                zb_copy(step - 1, side).wait_recv()
-                zsb[step, side] += zrb[step - 1, side] + yrecv[step, side]
-
-            @pl.when(step == 0)
-            def _():
-                zsb[step, side] += yrecv[step, side]
-
-            @pl.when(step < ZN - 1)
-            def _():
-                zb_copy(step, side).start()
+    def z_send(step, stream, late):
+        for way in range(2):
+            half = way if late else 1 - way
+            if step > 0 and (late or step > 1):
+                z_copy(step - 1, way, half, stream).wait_recv()
+                rows = STREAMS[stream]
+                zs[unit(step, way), half, rows, :] += zr[step - 1, way, half, rows, :]
+            z_copy(step, way, half, stream).start()
+
+    def z_end(stream):
+        rows = STREAMS[stream]
+        for half in range(2):
+            for way in range(2):
+                z_copy(3, way, half, stream).wait_recv()
+            zs[7, half, rows, :] += zr[3, 0, half, rows, :] + zr[3, 1, half, rows, :]
+
+    def yfin_copy():
+        return remote(yfin_src, yfin, yf_s, yf_r, y_peer)
 
     attend = Attention(lengths, q, keys, values, fk, fv, attn, qs, sc, sn, wc, mixed)
     for load in loads[4:8]:
         load.wait()
+    sum_one.two()
     attend.scores()
-    sum_one.two()
     for load in loads[8:10]:
         load.wait()
     attend.mix()
-    sum_one.three()
     loads[10].wait()
+
+    def next_units(u, carry):
+        core_stage(u + 2)
+        y_stage(u)
+        return carry
+
     core_stage(0)
     core_stage(1)
+    core_stage(2)
+    sum_one.three()
     y_stage(0)
+    z_send(0, 0, True)
+    z_send(0, 1, True)
+    lax.fori_loop(1, 3, next_units, 0)
+    z_send(1, 0, False)
+    z_send(1, 1, False)
+    y_add(0)
+    z_send(0, 2, True)
+    z_send(1, 0, True)
+    z_send(1, 1, True)
+    sum_one.four()
+    gradients()
+    lax.fori_loop(3, 5, next_units, 0)
+    y_add(1)
+    y_add(2)
+    z_send(1, 2, False)
+    z_send(1, 2, True)
     for load in loads[11:]:
         load.wait()
-
-    at_step = {
-        0: gradients,
-        1: gradient_sum,
-        2: update,
-        3: sum_two.two,
-        4: sum_two.three,
-    }
-
-    def ring(step, carry):
-        z_stage(step)
-
-        @pl.when(step < ZN - 1)
-        def _():
-            y_stage(step + 1)
-
-        @pl.when(step < ZN - 2)
-        def _():
-            core_stage(step + 2)
-
-        for when, work in at_step.items():
-            pl.when(step == when)(work)
-        return carry
-
-    lax.fori_loop(0, ZN, ring, 0)
-    for side in range(2):
-        yfin_copy(side).start()
-
+    z_send(2, 0, False)
+    z_send(2, 0, True)
+    z_send(2, 1, False)
+    z_send(2, 1, True)
+    gradient_sum()
+    next_units(5, 0)
+    lax.fori_loop(6, 8, lambda u, carry: (y_stage(u), carry)[1], 0)
+    y_add(3)
+    y_add(4)
+    z_send(2, 2, False)
+    z_send(2, 2, True)
+    update()
+    sum_two.two()
+    z_send(3, 0, False)
+    z_send(3, 0, True)
+    z_send(3, 1, False)
+    z_send(3, 1, True)
+    y_add(5)
+    y_add(6)
+    sum_two.three()
+    z_send(3, 2, False)
+    z_send(3, 2, True)
+    z_end(0)
+    for half in range(2):
+        yfin_src[half] = zs[7, half, STREAMS[0], :]
+    yfin_copy().start()
+    z_end(1)
     sum_two.four()
+    y_add(7)
+    z_end(2)
+    sum_two.five()
     u_high, u_low = two_terms(two_out[...])
     b_high, b_low = two_terms(b_out[...])
     left = jnp.concatenate([u_high, u_low, u_high], axis=1)
     right = jnp.concatenate([b_high, b_high, b_high, b_high, b_low, b_low], axis=0)
     delta = adapter_scale * dot(left, right)
 
-    for side in range(2):
-        rows_b = pl.ds(side * HALF + ROWS_A, ROWS_B)
-        summed[rows_b, :] = (
-            zsb[ZN - 1, side] + delta[side * HALF + ROWS_A : (side + 1) * HALF]
+    yfin_copy().wait_recv()
+    for half in range(2):
+        low, mid, high = half * HALF, half * HALF + FIRST, (half + 1) * HALF
+        summed[pl.ds(low, FIRST), :] = (
+            (zs[7, half, STREAMS[1], :] + yfin[half]) + delta[low:mid]
         ).astype(BF16)
-    for side in range(2):
-        yfin_copy(side).wait_recv()
-        rows_a = pl.ds(side * HALF, ROWS_A)
-        summed[rows_a, :] = (
-            (zsa[ZN - 1, side, 0] + yfin[side]) + delta[side * HALF : side * HALF + ROWS_A]
+        summed[pl.ds(mid, HALF - FIRST), :] = (
+            zs[7, half, STREAMS[2], :] + delta[mid:high]
         ).astype(BF16)
-
     back = lax.dot_general(
         attend.perm, summed[...], (((0,), (0,)), ((), ())), preferred_element_type=F32
     )
@@ -456,22 +472,16 @@
     for k in range(1, DP):
         grad_scatter(k).wait_send()
         grad_gather(k).wait_send()
-    for side in range(2):
-        yfin_copy(side).wait_send()
-
-    def drain(step, carry):
-        for side in range(2):
-            core_copy(step, side).wait_send()
-            y_copy(step, side).wait_send()
-
-            @pl.when(step < ZN - 1)
-            def _():
-                za_copy(step, side).wait_send()
-                zb_copy(step, side).wait_send()
-
-        return carry
-
-    lax.fori_loop(0, ZN, drain, 0)
+    yfin_copy().wait_send()
+    for u in range(8):
+        core_copy(u).wait_send()
+        y_copy(u).wait_send()
+    for way in range(2):
+        for stream in range(3):
+            z_copy(0, way, way, stream).wait_send()
+            for after in range(1, 4):
+                for half in range(2):
+                    z_copy(after, way, half, stream).wait_send()
 
 
 def step(*args):
@@ -481,9 +491,9 @@
     places = [pltpu.SMEM if arg.ndim == 1 else pltpu.VMEM for arg in args]
     small = [
         pltpu.VMEM((256, 128), F32),
-        pltpu.VMEM((7, 32, 128), F32),
-        pltpu.VMEM((32, 128), F32),
-        pltpu.VMEM((3, 32, 128), F32),
+        pltpu.VMEM((128, 128), F32),
+        pltpu.VMEM((128, 128), F32),
+        pltpu.VMEM((CHIPS - 1, 8, 128), F32),
         pltpu.VMEM((256, 128), F32),
     ]
     return pl.pallas_call(
@@ -500,25 +510,24 @@
             pltpu.VMEM((512, 128), F32),
             pltpu.VMEM((512, 256), BF16),
             pltpu.VMEM((512, 128), F32),
-            pltpu.VMEM((ZN, 2, 2, HALF, FEAT), F32),
-            pltpu.VMEM((ZN, 2, 2, HALF, FEAT), F32),
-            pltpu.VMEM((ZN, 2, ROWS_B, FEAT), F32),
-            pltpu.VMEM((ZN, 2, ROWS_B, FEAT), F32),
-            pltpu.VMEM((ZN, 2, 2, ROWS_A, FEAT), F32),
-            pltpu.VMEM((ZN - 1, 2, 2, ROWS_A, FEAT), F32),
-            pltpu.VMEM((ZN, 2, ROWS_B, FEAT), F32),
-            pltpu.VMEM((ZN - 1, 2, ROWS_B, FEAT), F32),
-            pltpu.VMEM((2, ROWS_A, FEAT), F32),
+            pltpu.VMEM((8, 2, ROWS, FEAT), F32),
+            pltpu.VMEM((8, 2, ROWS, FEAT), F32),
+            pltpu.VMEM((8, 2, HALF - FIRST, FEAT), F32),
+            pltpu.VMEM((8, 2, HALF - FIRST, FEAT), F32),
+            pltpu.VMEM((8, 2, HALF + FIRST, FEAT), F32),
+            pltpu.VMEM((4, 2, 2, HALF + FIRST, FEAT), F32),
+            pltpu.VMEM((2, FIRST, FEAT), F32),
+            pltpu.VMEM((2, FIRST, FEAT), F32),
             *small,
             pltpu.VMEM((128, FEAT), F32),
             pltpu.VMEM((7, 16, FEAT), F32),
             pltpu.VMEM((128, FEAT), F32),
             *small,
             dma((len(args),)),
-            dma((ZN, 2)), dma((ZN, 2)), dma((ZN, 2)), dma((ZN, 2)),
-            dma((ZN - 1, 2)), dma((ZN - 1, 2)), dma((ZN - 1, 2)), dma((ZN - 1, 2)),
-            dma((2,)), dma((2,)),
-            dma((48,)), dma((48,)),
+            dma((8,)), dma((8,)), dma((8,)), dma((8,)),
+            dma((4, 2, 2, 3)), dma((4, 2, 2, 3)),
+            dma, dma,
+            dma((78,)), dma((78,)),
         ],
         compiler_params=pltpu.CompilerParams(
             collective_id=0, has_side_effects=True, vmem_limit_bytes=64 * 1024 * 1024
@@ -528,23 +537,17 @@
 
 def hand_out_kernel(*refs):
     half = len(refs) // 2
-    copies = [
-        pltpu.make_async_copy(src, dst, refs[-1].at[i])
-        for i, (src, dst) in enumerate(zip(refs[:half], refs[half:-1]))
-    ]
-    for copy in copies:
-        copy.start()
-    for copy in copies:
-        copy.wait()
+    for src, dst in zip(refs[:half], refs[half:]):
+        dst[...] = src[...]
 
 
 def hand_out(*args):
+    vmem = pl.BlockSpec(memory_space=pltpu.VMEM)
     return pl.pallas_call(
         hand_out_kernel,
         out_shape=tuple(jax.ShapeDtypeStruct(arg.shape, arg.dtype) for arg in args),
-        in_specs=[pl.BlockSpec(memory_space=pl.ANY)] * len(args),
-        out_specs=(pl.BlockSpec(memory_space=pltpu.HBM),) * len(args),
-        scratch_shapes=[pltpu.SemaphoreType.DMA((len(args),))],
+        in_specs=[vmem] * len(args),
+        out_specs=(vmem,) * len(args),
         compiler_params=pltpu.CompilerParams(vmem_limit_bytes=64 * 1024 * 1024),
     )(*args)
 

time: 88.4 us -> 61.5 us (0.70)
  the two profiles are of different devices: /device:TPU:32 before, /device:TPU:1 now
where the time goes in v3:
time: 61.5 us; the launch traced here: 61.4 us
  Pallas kernels  60.7 us (99%)
  between operations  0.65 us (1%)
    pallas_call x1, Pallas kernels, step(): pl.pallas_call(step_kernel, out_shape=(jax.ShapeDtypeStruct((ROWS, FEAT),...  58.9 us
    pallas_call x1, Pallas kernels, hand_out(): pl.pallas_call(hand_out_kernel, out_shape=tuple((jax.ShapeDtypeStruct(arg...  1.85 us

profile of v3, /device:TPU:1, one launch (start us, length us, event | category | flops | bytes accessed | tf_op | source)
XLA Modules:
  0.0 61.4 jit_solution(2707629331910049552)
XLA Ops:
  0.6 58.9 %shard_map.198 = (bf16[256,256]{1,0:T(8,128)(2,1)}, f32[64,256]{1,0:T(8,128)}, f32[64,256]{1,0:T(8,128)}, f32[64,256]{1,0:T(8,128)}, f32[64,256]{1,0:T(8,128)}, /*index=5*/f32[64,256]{1,0:T(8,128)}, f32[64,256]{1,0:T(8,128)}) custom-call(bf16[256,256]{1,0:T(8,128)(2,1)} %x_h.1, bf16[256,256]{1,0:T(8,128)(2,1)} %dy_h.1, f32[64,256]{1,0:T(8,128)} %bitcast.11, ...), custom_call_target="tpu_custom_call" | custom-call | tf_op jit(solution)/shard_map/pallas_call | solution.py:499
  59.5 1.9 %shard_map.199 = (bf16[256,256]{1,0:T(8,128)(2,1)}, f32[64,256]{1,0:T(8,128)}, f32[64,256]{1,0:T(8,128)}, f32[64,256]{1,0:T(8,128)}, f32[64,256]{1,0:T(8,128)}, /*index=5*/f32[64,256]{1,0:T(8,128)}, f32[64,256]{1,0:T(8,128)}) custom-call(bf16[256,256]{1,0:T(8,128)(2,1)} %get-tuple-element.21.refs_0_, f32[64,256]{1,0:T(8,128)} %get-tuple-element.22.refs_1_, ...), custom_call_target="tpu_custom_call" | custom-call | tf_op jit(solution)/shard_map/pallas_call | solution.py:546

commit v4 on v3

--- a/solution.py
+++ b/solution.py
@@ -56,13 +56,14 @@
 
 
 class Attention:
-    def __init__(self, lengths, q, k, v, fk, fv, out, qs, sc, sn, wc, mixed):
+    def __init__(self, lengths, q, k, v, fk, fv, out, qs, sc, sn, mixed):
         self.lengths, self.q, self.k, self.v, self.fk, self.fv = lengths, q, k, v, fk, fv
-        self.out, self.qs, self.sc, self.sn, self.wc, self.mixed = out, qs, sc, sn, wc, mixed
+        self.out, self.qs, self.sc, self.sn, self.mixed = out, qs, sc, sn, mixed
         self.pairs = k.shape[0] // 2
         i0 = lax.broadcasted_iota(jnp.int32, (ROWS, ROWS), 0)
         i1 = lax.broadcasted_iota(jnp.int32, (ROWS, ROWS), 1)
         self.perm = jnp.where(i1 == (i0 % 4) * 64 + i0 // 4, 1.0, 0.0).astype(BF16)
+        self.back = jnp.where(i0 == (i1 % 4) * 64 + i1 // 4, 1.0, 0.0).astype(BF16)
 
     def scores(self):
         pairs, qs, sc, sn = self.pairs, self.qs, self.sc, self.sn
@@ -87,7 +88,7 @@
             sc[at, :] = jnp.where((col >= start) & (col < stop), s, -jnp.inf)
             return carry
 
-        lax.fori_loop(0, pairs, one_pair, 0, unroll=8)
+        lax.fori_loop(0, pairs, one_pair, 0, unroll=32)
 
         nrow = lax.broadcasted_iota(jnp.int32, (256, 128), 0)
         ncol = lax.broadcasted_iota(jnp.int32, (256, 128), 1)
@@ -99,7 +100,8 @@
             sn[part, :] = jnp.where(new_live, s, -jnp.inf)
 
     def mix(self):
-        pairs, sc, sn, wc, mixed = self.pairs, self.sc, self.sn, self.wc, self.mixed
+        sc, sn, mixed = self.sc, self.sn, self.mixed
+        pairs = self.pairs
         fv = dot(self.perm, self.fv[...]).astype(BF16)
         for block in range(8):
             part = pl.ds(block * 64, 64)
@@ -110,27 +112,27 @@
             e, m = jnp.exp(s - largest), jnp.exp(n - largest)
             total = jnp.sum(e, axis=1, keepdims=True) + jnp.sum(m, axis=1, keepdims=True)
             scale = 1.0 / total
-            wc[part, :] = (e * scale).astype(BF16)
+            weights = (e * scale).astype(BF16)
             where_new = (block // 4) * 128
-            mixed[part, :] = dot((m * scale).astype(BF16), fv[where_new : where_new + 128])
-
-        def one_pair(p, carry):
-            values = self.v[pl.ds(2 * p, 2)].reshape(256, 128)
-            at = pl.ds(pl.multiple_of(p * 16, 16), 16)
-            mixed[at, :] += dot(wc[at, :], values)
-            return carry
-
-        lax.fori_loop(0, pairs, one_pair, 0, unroll=8)
+            new = dot((m * scale).astype(BF16), fv[where_new : where_new + 128])
+            for i in range(4):
+                p = block * 4 + i
+                values = self.v[2 * p : 2 * p + 2].reshape(256, 128)
+                mixed[p * 16 : p * 16 + 16, :] = (
+                    dot(weights[i * 16 : i * 16 + 16], values) + new[i * 16 : i * 16 + 16]
+                )
         o = mixed[...].reshape(pairs, 16, 128)
-        self.out[:, :128] = o[:, :8].reshape(ROWS, 128).astype(BF16)
-        self.out[:, 128:] = o[:, 8:].reshape(ROWS, 128).astype(BF16)
+        o = jnp.concatenate(
+            [o[:, :8].reshape(ROWS, 128), o[:, 8:].reshape(ROWS, 128)], axis=1
+        ).astype(BF16)
+        self.out[...] = dot(self.back, o).astype(BF16)
 
 
 def step_kernel(
     x_h, dy_h, a_h, b_h, len_h, q_h, fk_h, k_h, fv_h, v_h, w_h, am_h, av_h, bm_h, bv_h,
     dec, a_out, b_out, am_out, av_out, bm_out, bv_out,
     x, dy, a_ref, b_ref, lengths, q, fk, keys, fv, values, w, am_ref, av_ref, bm_ref, bv_ref,
-    attn, summed, qs, sc, sn, wc, mixed,
+    attn, base, right, qs, sc, sn, mixed,
     csend, crecv, ysend, yrecv, zs, zr, yfin_src, yfin,
     one_in, one_core, one_half, one_recv, one_out,
     grad, grad_r, grad_out,
@@ -150,19 +152,19 @@
     chip_peers = [(d, lax.rem(chip + k, CHIPS) * 2 + c) for k in range(1, CHIPS)]
     dp_peers = [(lax.rem(d + k, DP), t) for k in range(1, DP)]
 
+    barrier = pltpu.get_barrier_semaphore()
+    everyone = chip_peers[7:] + chip_peers[:7][::-1] + dp_peers + [core_peer]
+    for peer in everyone:
+        pl.semaphore_signal(barrier, inc=1, device_id=peer, device_id_type=MESH)
+
     here = (x, dy, a_ref, b_ref, lengths, q, fk, keys, fv, values, w, am_ref, av_ref, bm_ref, bv_ref)
     there = (x_h, dy_h, a_h, b_h, len_h, q_h, fk_h, k_h, fv_h, v_h, w_h, am_h, av_h, bm_h, bv_h)
     loads = [
         pltpu.make_async_copy(src, dst, in_sem.at[i])
         for i, (src, dst) in enumerate(zip(there, here))
     ]
-    for load in loads:
+    for load in loads[:8]:
         load.start()
-
-    barrier = pltpu.get_barrier_semaphore()
-    everyone = chip_peers + [core_peer] + dp_peers
-    for peer in everyone:
-        pl.semaphore_signal(barrier, inc=1, device_id=peer, device_id_type=MESH)
 
     def remote(src, dst, send_sem, recv_sem, peer):
         return pltpu.make_async_remote_copy(
@@ -246,6 +248,8 @@
 
     for load in loads[:4]:
         load.wait()
+    for load in loads[8:11]:
+        load.start()
     a_high, a_low = two_terms(a_ref[...])
     b_high, b_low = two_terms(b_ref[...])
     one_in[...] = jnp.concatenate(
@@ -340,7 +344,6 @@
             zs[u, half, STREAMS[0], :] = other[low:mid]
             zs[u, half, STREAMS[1], :] = own[low:mid]
             zs[u, half, STREAMS[2], :] = own[mid:high]
-        y_copy(u).start()
 
     def y_add(u):
         y_copy(u).wait_recv()
@@ -375,13 +378,42 @@
                 z_copy(3, way, half, stream).wait_recv()
             zs[7, half, rows, :] += zr[3, 0, half, rows, :] + zr[3, 1, half, rows, :]
 
+    def rest():
+        sum_one.finish()
+        for k in range(1, DP):
+            grad_scatter(k).wait_send()
+            grad_gather(k).wait_send()
+        b_high, b_low = two_terms(b_out[...])
+        right[...] = jnp.concatenate([b_high, b_high, b_high, b_high, b_low, b_low], axis=0)
+
+    def base_sum():
+        yfin_copy().wait_recv()
+        for half in range(2):
+            low, mid = half * HALF, half * HALF + FIRST
+            base[pl.ds(low, FIRST), :] = zs[7, half, STREAMS[1], :] + yfin[half]
+            base[pl.ds(mid, HALF - FIRST), :] = zs[7, half, STREAMS[2], :]
+
+    def drain():
+        yfin_copy().wait_send()
+        for u in range(8):
+            core_copy(u).wait_send()
+            y_copy(u).wait_send()
+        for way in range(2):
+            for stream in range(3):
+                z_copy(0, way, way, stream).wait_send()
+                for after in range(1, 4):
+                    for half in range(2):
+                        z_copy(after, way, half, stream).wait_send()
+
     def yfin_copy():
         return remote(yfin_src, yfin, yf_s, yf_r, y_peer)
 
-    attend = Attention(lengths, q, keys, values, fk, fv, attn, qs, sc, sn, wc, mixed)
+    attend = Attention(lengths, q, keys, values, fk, fv, attn, qs, sc, sn, mixed)
     for load in loads[4:8]:
         load.wait()
     sum_one.two()
+    for load in loads[11:]:
+        load.start()
     attend.scores()
     for load in loads[8:10]:
         load.wait()
@@ -396,13 +428,16 @@
     core_stage(0)
     core_stage(1)
     core_stage(2)
-    sum_one.three()
     y_stage(0)
+    y_copy(0).start()
     z_send(0, 0, True)
     z_send(0, 1, True)
+    sum_one.three()
     lax.fori_loop(1, 3, next_units, 0)
+    y_copy(1).start()
     z_send(1, 0, False)
     z_send(1, 1, False)
+    y_copy(2).start()
     y_add(0)
     z_send(0, 2, True)
     z_send(1, 0, True)
@@ -410,6 +445,8 @@
     sum_one.four()
     gradients()
     lax.fori_loop(3, 5, next_units, 0)
+    y_copy(3).start()
+    y_copy(4).start()
     y_add(1)
     y_add(2)
     z_send(1, 2, False)
@@ -422,7 +459,10 @@
     z_send(2, 1, True)
     gradient_sum()
     next_units(5, 0)
+    y_copy(5).start()
     lax.fori_loop(6, 8, lambda u, carry: (y_stage(u), carry)[1], 0)
+    y_copy(6).start()
+    y_copy(7).start()
     y_add(3)
     y_add(4)
     z_send(2, 2, False)
@@ -433,55 +473,27 @@
     z_send(3, 0, True)
     z_send(3, 1, False)
     z_send(3, 1, True)
+    z_end(0)
+    for half in range(2):
+        yfin_src[half] = zs[7, half, STREAMS[0], :]
+    yfin_copy().start()
     y_add(5)
     y_add(6)
     sum_two.three()
     z_send(3, 2, False)
     z_send(3, 2, True)
-    z_end(0)
-    for half in range(2):
-        yfin_src[half] = zs[7, half, STREAMS[0], :]
-    yfin_copy().start()
+    rest()
     z_end(1)
     sum_two.four()
     y_add(7)
     z_end(2)
+    base_sum()
+    drain()
     sum_two.five()
     u_high, u_low = two_terms(two_out[...])
-    b_high, b_low = two_terms(b_out[...])
     left = jnp.concatenate([u_high, u_low, u_high], axis=1)
-    right = jnp.concatenate([b_high, b_high, b_high, b_high, b_low, b_low], axis=0)
-    delta = adapter_scale * dot(left, right)
-
-    yfin_copy().wait_recv()
-    for half in range(2):
-        low, mid, high = half * HALF, half * HALF + FIRST, (half + 1) * HALF
-        summed[pl.ds(low, FIRST), :] = (
-            (zs[7, half, STREAMS[1], :] + yfin[half]) + delta[low:mid]
-        ).astype(BF16)
-        summed[pl.ds(mid, HALF - FIRST), :] = (
-            zs[7, half, STREAMS[2], :] + delta[mid:high]
-        ).astype(BF16)
-    back = lax.dot_general(
-        attend.perm, summed[...], (((0,), (0,)), ((), ())), preferred_element_type=F32
-    )
-    dec[...] = back.astype(BF16)
-
-    sum_one.finish()
+    dec[...] = (base[...] + adapter_scale * dot(left, right[...])).astype(BF16)
     sum_two.finish()
-    for k in range(1, DP):
-        grad_scatter(k).wait_send()
-        grad_gather(k).wait_send()
-    yfin_copy().wait_send()
-    for u in range(8):
-        core_copy(u).wait_send()
-        y_copy(u).wait_send()
-    for way in range(2):
-        for stream in range(3):
-            z_copy(0, way, way, stream).wait_send()
-            for after in range(1, 4):
-                for half in range(2):
-                    z_copy(after, way, half, stream).wait_send()
 
 
 def step(*args):
@@ -504,11 +516,11 @@
         scratch_shapes=[
             *[place(arg.shape, arg.dtype) for place, arg in zip(places, args)],
             pltpu.VMEM((ROWS, FEAT), BF16),
-            pltpu.VMEM((ROWS, FEAT), BF16),
+            pltpu.VMEM((ROWS, FEAT), F32),
+            pltpu.VMEM((6 * RANK, FEAT), BF16),
             pltpu.VMEM((512, 128), BF16),
             pltpu.VMEM((512, 256), F32),
             pltpu.VMEM((512, 128), F32),
-            pltpu.VMEM((512, 256), BF16),
             pltpu.VMEM((512, 128), F32),
             pltpu.VMEM((8, 2, ROWS, FEAT), F32),
             pltpu.VMEM((8, 2, ROWS, FEAT), F32),
@@ -530,25 +542,31 @@
             dma((78,)), dma((78,)),
         ],
         compiler_params=pltpu.CompilerParams(
-            collective_id=0, has_side_effects=True, vmem_limit_bytes=64 * 1024 * 1024
+            collective_id=0, has_side_effects=True, vmem_limit_bytes=52 * 1024 * 1024
         ),
-    )(*args)
+    )(*[pltpu.with_memory_space_constraint(arg, pltpu.HBM) for arg in args])
 
 
 def hand_out_kernel(*refs):
     half = len(refs) // 2
-    for src, dst in zip(refs[:half], refs[half:]):
-        dst[...] = src[...]
+    copies = [
+        pltpu.make_async_copy(src, dst, refs[-1].at[i])
+        for i, (src, dst) in enumerate(zip(refs[:half], refs[half:-1]))
+    ]
+    for copy in copies:
+        copy.start()
+    for copy in copies:
+        copy.wait()
 
 
 def hand_out(*args):
-    vmem = pl.BlockSpec(memory_space=pltpu.VMEM)
     return pl.pallas_call(
         hand_out_kernel,
         out_shape=tuple(jax.ShapeDtypeStruct(arg.shape, arg.dtype) for arg in args),
-        in_specs=[vmem] * len(args),
-        out_specs=(vmem,) * len(args),
-        compiler_params=pltpu.CompilerParams(vmem_limit_bytes=64 * 1024 * 1024),
+        in_specs=[pl.BlockSpec(memory_space=pltpu.VMEM)] * len(args),
+        out_specs=(pl.BlockSpec(memory_space=pltpu.HBM),) * len(args),
+        scratch_shapes=[pltpu.SemaphoreType.DMA((len(args),))],
+        compiler_params=pltpu.CompilerParams(vmem_limit_bytes=4 * 1024 * 1024),
     )(*args)
 
 

time: 61.5 us -> 57.7 us (0.938)
  Pallas kernels: 60.7 us -> 57 us
    pallas_call x1, Pallas kernels: 58.9 us -> 56.1 us  [step(): pl.pallas_call(step_kernel, out_shape=(jax.ShapeDtypeStruct((ROWS, FEAT),...]
    pallas_call x1, Pallas kernels: 1.85 us -> 0.84 us  [hand_out(): pl.pallas_call(hand_out_kernel, out_shape=tuple((jax.ShapeDtypeStruct(arg...]
where the time goes in v4:
time: 57.7 us; the launch traced here: 57.6 us
  Pallas kernels  57 us (99%)
  between operations  0.65 us (1%)
    pallas_call x1, Pallas kernels, step(): pl.pallas_call(step_kernel, out_shape=(jax.ShapeDtypeStruct((ROWS, FEAT),...  56.1 us

profile of v4, /device:TPU:1, one launch (start us, length us, event | category | flops | bytes accessed | tf_op | source)
XLA Modules:
  0.0 57.6 jit_solution(17140200283502635860)
XLA Ops:
  0.6 56.1 %shard_map.198 = (bf16[256,256]{1,0:T(8,128)(2,1)S(1)}, f32[64,256]{1,0:T(8,128)S(1)}, f32[64,256]{1,0:T(8,128)S(1)}, f32[64,256]{1,0:T(8,128)S(1)}, f32[64,256]...) custom-call(bf16[256,256]{1,0:T(8,128)(2,1)} %x_h.1, bf16[256,256]{1,0:T(8,128)(2,1)} %dy_h.1, ...), custom_call_target="tpu_custom_call" | custom-call | tf_op jit(solution)/shard_map/pallas_call | solution.py:511
  56.8 0.8 %shard_map.199 = (bf16[256,256]{1,0:T(8,128)(2,1)}, f32[64,256]{1,0:T(8,128)}, f32[64,256]{1,0:T(8,128)}, f32[64,256]{1,0:T(8,128)}, f32[64,256]{1,0:T(8,128)}, /*index=5*/f32[64,256]{1,0:T(8,128)}, f32[64,256]{1,0:T(8,128)}) custom-call(bf16[256,256]{1,0:T(8,128)(2,1)S(1)} %get-tuple-element.21.refs_0_, f32[64,256]{1,0:T(8,128)S(1)} %get-tuple-element.22.refs_1_, ...), custom_call_target="tpu_custom_call" | custom-call | tf_op jit(solution)/shard_map/pallas_call | solution.py:563

commit v5 on v4

--- a/solution.py
+++ b/solution.py
@@ -177,20 +177,24 @@
         )
 
     class TensorSum:
-        def __init__(self, src, core_recv, half, recv, out, first):
+        def __init__(self, src, core_recv, half, recv, out, first, pairs):
             self.src, self.core_recv, self.half = src, core_recv, half
-            self.recv, self.out, self.first = recv, out, first
-            self.mine = pl.ds(pl.multiple_of(c * 128, 128), 128)
-            self.theirs = pl.ds(pl.multiple_of((1 - c) * 128, 128), 128)
-            self.part = pl.ds(pl.multiple_of(chip * 8, 8), 8)
-            self.here = pl.ds(pl.multiple_of(c * 128 + chip * 8, 8), 8)
+            self.recv, self.out, self.first, self.pairs = recv, out, first, pairs
+            rows = half.shape[0]
+            part = z if pairs else chip
+            self.mine = pl.ds(pl.multiple_of(c * rows, rows), rows)
+            self.theirs = pl.ds(pl.multiple_of((1 - c) * rows, rows), rows)
+            self.part = pl.ds(pl.multiple_of(part * 8, 8), 8)
+            self.here = pl.ds(pl.multiple_of(c * rows + part * 8, 8), 8)
+            self.back = range(2, CHIPS, 2) if pairs else range(1, CHIPS)
 
         def core_scatter(self):
             i = self.first
             return remote(self.src.at[self.theirs], self.core_recv, t_s.at[i], t_r.at[i], core_peer)
 
         def scatter(self, k):
-            part = pl.ds(pl.multiple_of(lax.rem(chip + k, CHIPS) * 8, 8), 8)
+            to = lax.rem(chip + k, CHIPS)
+            part = pl.ds(pl.multiple_of((to // 2 if self.pairs else to) * 8, 8), 8)
             i = self.first + k
             return remote(
                 self.half.at[part], self.recv.at[k - 1], t_s.at[i], t_r.at[i], chip_peers[k - 1]
@@ -225,11 +229,11 @@
             for k in range(1, CHIPS):
                 total = total + self.recv[k - 1]
             self.out[self.here, :] = total
-            for k in range(1, CHIPS):
+            for k in self.back:
                 self.gather(k).start()
 
         def four(self):
-            for k in range(1, CHIPS):
+            for k in self.back:
                 self.gather(k).wait_recv()
             self.core_gather().start()
 
@@ -241,10 +245,11 @@
             self.core_gather().wait_send()
             for k in range(1, CHIPS):
                 self.scatter(k).wait_send()
+            for k in self.back:
                 self.gather(k).wait_send()
 
-    sum_one = TensorSum(one_in, one_core, one_half, one_recv, one_out, 0)
-    sum_two = TensorSum(two_in, two_core, two_half, two_recv, two_out, 32)
+    sum_one = TensorSum(one_in, one_core, one_half, one_recv, one_out, 0, False)
+    sum_two = TensorSum(two_in, two_core, two_half, two_recv, two_out, 32, True)
 
     for load in loads[:4]:
         load.wait()
@@ -304,7 +309,15 @@
         )
         a_out[...], am_out[...], av_out[...] = new_a, a_one, a_two
         high, low = two_terms(new_a)
-        two_in[...] = dot_t(attn[...], jnp.concatenate([high, low], axis=0))
+        none = jnp.zeros_like(high)
+        first, second = attn[:HALF, :], attn[HALF:, :]
+        two_in[...] = (
+            dot_t(first, jnp.concatenate([high, none], axis=0))
+            + dot_t(second, jnp.concatenate([none, high], axis=0))
+        ) + (
+            dot_t(first, jnp.concatenate([low, none], axis=0))
+            + dot_t(second, jnp.concatenate([none, low], axis=0))
+        )
         sum_two.one()
         new_b, b_one, b_two = apply_adam_step(
             b_ref[...], bm_ref[...], bv_ref[...], grad_out[RANK:, :]
@@ -384,7 +397,9 @@
             grad_scatter(k).wait_send()
             grad_gather(k).wait_send()
         b_high, b_low = two_terms(b_out[...])
-        right[...] = jnp.concatenate([b_high, b_high, b_high, b_high, b_low, b_low], axis=0)
+        none = jnp.zeros_like(b_high)
+        right[0] = jnp.concatenate([b_high, none, b_high, none, b_low, none], axis=0)
+        right[1] = jnp.concatenate([none, b_high, none, b_high, none, b_low], axis=0)
 
     def base_sum():
         yfin_copy().wait_recv()
@@ -460,31 +475,31 @@
     gradient_sum()
     next_units(5, 0)
     y_copy(5).start()
-    lax.fori_loop(6, 8, lambda u, carry: (y_stage(u), carry)[1], 0)
-    y_copy(6).start()
-    y_copy(7).start()
     y_add(3)
     y_add(4)
     z_send(2, 2, False)
     z_send(2, 2, True)
     update()
+    lax.fori_loop(6, 8, lambda u, carry: (y_stage(u), carry)[1], 0)
+    y_copy(6).start()
+    y_copy(7).start()
     sum_two.two()
     z_send(3, 0, False)
     z_send(3, 0, True)
     z_send(3, 1, False)
     z_send(3, 1, True)
+    sum_two.three()
     z_end(0)
     for half in range(2):
         yfin_src[half] = zs[7, half, STREAMS[0], :]
     yfin_copy().start()
     y_add(5)
     y_add(6)
-    sum_two.three()
     z_send(3, 2, False)
     z_send(3, 2, True)
     rest()
+    sum_two.four()
     z_end(1)
-    sum_two.four()
     y_add(7)
     z_end(2)
     base_sum()
@@ -492,7 +507,9 @@
     sum_two.five()
     u_high, u_low = two_terms(two_out[...])
     left = jnp.concatenate([u_high, u_low, u_high], axis=1)
-    dec[...] = (base[...] + adapter_scale * dot(left, right[...])).astype(BF16)
+    for half in range(2):
+        rows = pl.ds(half * HALF, HALF)
+        dec[rows, :] = (base[rows, :] + adapter_scale * dot(left, right[half])).astype(BF16)
     sum_two.finish()
 
 
@@ -517,7 +534,7 @@
             *[place(arg.shape, arg.dtype) for place, arg in zip(places, args)],
             pltpu.VMEM((ROWS, FEAT), BF16),
             pltpu.VMEM((ROWS, FEAT), F32),
-            pltpu.VMEM((6 * RANK, FEAT), BF16),
+            pltpu.VMEM((2, 6 * RANK, FEAT), BF16),
             pltpu.VMEM((512, 128), BF16),
             pltpu.VMEM((512, 256), F32),
             pltpu.VMEM((512, 128), F32),
@@ -534,7 +551,11 @@
             pltpu.VMEM((128, FEAT), F32),
             pltpu.VMEM((7, 16, FEAT), F32),
             pltpu.VMEM((128, FEAT), F32),
-            *small,
+            pltpu.VMEM((128, 128), F32),
+            pltpu.VMEM((64, 128), F32),
+            pltpu.VMEM((64, 128), F32),
+            pltpu.VMEM((CHIPS - 1, 8, 128), F32),
+            pltpu.VMEM((128, 128), F32),
             dma((len(args),)),
             dma((8,)), dma((8,)), dma((8,)), dma((8,)),
             dma((4, 2, 2, 3)), dma((4, 2, 2, 3)),

time: 57.7 us -> 55.9 us (0.969)
  Pallas kernels: 57 us -> 55.2 us
    pallas_call x1, Pallas kernels: 56.1 us -> 54.3 us  [step(): pl.pallas_call(step_kernel, out_shape=(jax.ShapeDtypeStruct((ROWS, FEAT),...]
where the time goes in v5:
time: 55.9 us; the launch traced here: 55.8 us
  Pallas kernels  55.2 us (99%)
  between operations  0.65 us (1%)
    pallas_call x1, Pallas kernels, step(): pl.pallas_call(step_kernel, out_shape=(jax.ShapeDtypeStruct((ROWS, FEAT),...  54.3 us

profile of v5, /device:TPU:1, one launch (start us, length us, event | category | flops | bytes accessed | tf_op | source)
XLA Modules:
  0.0 55.8 jit_solution(10234693888543767011)
XLA Ops:
  0.6 54.3 %shard_map.198 = (bf16[256,256]{1,0:T(8,128)(2,1)S(1)}, f32[64,256]{1,0:T(8,128)S(1)}, f32[64,256]{1,0:T(8,128)S(1)}, f32[64,256]{1,0:T(8,128)S(1)}, f32[64,256]...) custom-call(bf16[256,256]{1,0:T(8,128)(2,1)} %x_h.1, bf16[256,256]{1,0:T(8,128)(2,1)} %dy_h.1, ...), custom_call_target="tpu_custom_call" | custom-call | tf_op jit(solution)/shard_map/pallas_call | solution.py:528
  55.0 0.8 %shard_map.199 = (bf16[256,256]{1,0:T(8,128)(2,1)}, f32[64,256]{1,0:T(8,128)}, f32[64,256]{1,0:T(8,128)}, f32[64,256]{1,0:T(8,128)}, f32[64,256]{1,0:T(8,128)}, /*index=5*/f32[64,256]{1,0:T(8,128)}, f32[64,256]{1,0:T(8,128)}) custom-call(bf16[256,256]{1,0:T(8,128)(2,1)S(1)} %get-tuple-element.21.refs_0_, f32[64,256]{1,0:T(8,128)S(1)} %get-tuple-element.22.refs_1_, ...), custom_call_target="tpu_custom_call" | custom-call | tf_op jit(solution)/shard_map/pallas_call | solution.py:584

commit v6 on v5

--- a/solution.py
+++ b/solution.py
@@ -181,11 +181,13 @@
             self.src, self.core_recv, self.half = src, core_recv, half
             self.recv, self.out, self.first, self.pairs = recv, out, first, pairs
             rows = half.shape[0]
+            size = recv.shape[1]
             part = z if pairs else chip
             self.mine = pl.ds(pl.multiple_of(c * rows, rows), rows)
             self.theirs = pl.ds(pl.multiple_of((1 - c) * rows, rows), rows)
-            self.part = pl.ds(pl.multiple_of(part * 8, 8), 8)
-            self.here = pl.ds(pl.multiple_of(c * rows + part * 8, 8), 8)
+            self.size = size
+            self.part = pl.ds(pl.multiple_of(part * size, size), size)
+            self.here = pl.ds(pl.multiple_of(c * rows + part * size, size), size)
             self.back = range(2, CHIPS, 2) if pairs else range(1, CHIPS)
 
         def core_scatter(self):
@@ -194,7 +196,8 @@
 
         def scatter(self, k):
             to = lax.rem(chip + k, CHIPS)
-            part = pl.ds(pl.multiple_of((to // 2 if self.pairs else to) * 8, 8), 8)
+            size = self.size
+            part = pl.ds(pl.multiple_of((to // 2 if self.pairs else to) * size, size), size)
             i = self.first + k
             return remote(
                 self.half.at[part], self.recv.at[k - 1], t_s.at[i], t_r.at[i], chip_peers[k - 1]
@@ -248,7 +251,7 @@
             for k in self.back:
                 self.gather(k).wait_send()
 
-    sum_one = TensorSum(one_in, one_core, one_half, one_recv, one_out, 0, False)
+    sum_one = TensorSum(one_in, one_core, one_half, one_recv, one_out, 0, True)
     sum_two = TensorSum(two_in, two_core, two_half, two_recv, two_out, 32, True)
 
     for load in loads[:4]:
@@ -469,8 +472,8 @@
     for load in loads[11:]:
         load.wait()
     z_send(2, 0, False)
+    z_send(2, 1, False)
     z_send(2, 0, True)
-    z_send(2, 1, False)
     z_send(2, 1, True)
     gradient_sum()
     next_units(5, 0)
@@ -522,7 +525,7 @@
         pltpu.VMEM((256, 128), F32),
         pltpu.VMEM((128, 128), F32),
         pltpu.VMEM((128, 128), F32),
-        pltpu.VMEM((CHIPS - 1, 8, 128), F32),
+        pltpu.VMEM((CHIPS - 1, 16, 128), F32),
         pltpu.VMEM((256, 128), F32),
     ]
     return pl.pallas_call(

time: 55.9 us -> 56 us (level)
  no operation moved by 1% of the time
where the time goes in v6:
time: 56 us; the launch traced here: 55.9 us
  Pallas kernels  55.2 us (99%)
  between operations  0.65 us (1%)
    pallas_call x1, Pallas kernels, step(): pl.pallas_call(step_kernel, out_shape=(jax.ShapeDtypeStruct((ROWS, FEAT),...  54.4 us

profile of v6, /device:TPU:1, one launch (start us, length us, event | category | flops | bytes accessed | tf_op | source)
XLA Modules:
  0.0 55.9 jit_solution(17088466623370520571)
XLA Ops:
  0.6 54.4 %shard_map.198 = (bf16[256,256]{1,0:T(8,128)(2,1)S(1)}, f32[64,256]{1,0:T(8,128)S(1)}, f32[64,256]{1,0:T(8,128)S(1)}, f32[64,256]{1,0:T(8,128)S(1)}, f32[64,256]...) custom-call(bf16[256,256]{1,0:T(8,128)(2,1)} %x_h.1, bf16[256,256]{1,0:T(8,128)(2,1)} %dy_h.1, ...), custom_call_target="tpu_custom_call" | custom-call | tf_op jit(solution)/shard_map/pallas_call | solution.py:531
  55.0 0.8 %shard_map.199 = (bf16[256,256]{1,0:T(8,128)(2,1)}, f32[64,256]{1,0:T(8,128)}, f32[64,256]{1,0:T(8,128)}, f32[64,256]{1,0:T(8,128)}, f32[64,256]{1,0:T(8,128)}, /*index=5*/f32[64,256]{1,0:T(8,128)}, f32[64,256]{1,0:T(8,128)}) custom-call(bf16[256,256]{1,0:T(8,128)(2,1)S(1)} %get-tuple-element.21.refs_0_, f32[64,256]{1,0:T(8,128)S(1)} %get-tuple-element.22.refs_1_, ...), custom_call_target="tpu_custom_call" | custom-call | tf_op jit(solution)/shard_map/pallas_call | solution.py:587
